TPU v7x, 32 devices: a whole 2x2x4 slice. The times are simulated.
32 devices in a mesh: groups: 2 (over y), space: 4 (over z), test: 4 (over x, core).
Axes of the slice: x: 2, y: 2, z: 4, core: 2. Of those that a mesh axis runs over, the one named last changes fastest.
Arguments:
- log_k: bfloat16 [384, 288, 128], P(('groups', 'space')), parts along dimension 0, may hold values from -1.5 to 1.5
- heads: bfloat16 [4, 384, 288, 128], P('test', ('groups', 'space')), parts along dimension 1, may hold values from -6 to 6
- warm_adjoint: bfloat16 [4, 384, 288, 128], P('test', ('groups', 'space')), parts along dimension 1, may hold values from -6 to 6
- obs_columns: int32 [4, 128], P('test', 'groups'), parts along dimension 1, may hold values from 0 to 55295
- obs_residuals: float32 [4, 128, 128], P('test', 'groups'), parts along dimension 1, may hold values from -18 to 18
- well_columns: int32 [8], P(('groups', 'test')), parts along dimension 0, may hold values from 0 to 55295
Outputs:
- prior_gradient: float32 [384, 288, 128], P(('groups', 'space'), 'test'), parts along dimension 0
There are 2 independent parts, one for each index of `groups`. A program takes and returns all parts, laid end to end along the dimension named above; each array names one. Nothing has to cross between parts.
Inputs may be any that keep to these rules, and one draw needn't show every extreme that they name: `obs_columns`: x * 288 + y of the borehole's cell column. `well_columns`: x * 288 + y of the well's cell column.
All inputs are finite; a program needn't handle non-finite values.
Results may differ from a plain program's by a relative error of at most 0.0003.
Values may be sent and summed in bfloat16 or wider, within the bound.
A program may use at most 128 MiB of HBM per device.

v0:
```python
import jax
import jax.numpy as jnp
from jax import lax
from jax.sharding import PartitionSpec as P

ITERS = 2


prior_gain = 5.0
range_squared = 4.0


def with_halo(cells, sides, width):
    for axis, dim in sides:
        count = lax.axis_size(axis)
        ends = count - 1
        head = lax.slice_in_dim(cells, 0, width, axis=dim)
        tail = lax.slice_in_dim(cells, cells.shape[dim] - width, cells.shape[dim], axis=dim)
        cells = jnp.concatenate(
            [
                lax.ppermute(tail, axis, [(i, (i + 1) % count) for i in range(ends)]),
                cells,
                lax.ppermute(head, axis, [((i + 1) % count, i) for i in range(ends)]),
            ],
            axis=dim,
        )
    return cells


def neighbours(padded):
    return [
        padded[2:, 1:-1, 1:-1],
        padded[:-2, 1:-1, 1:-1],
        padded[1:-1, 2:, 1:-1],
        padded[1:-1, :-2, 1:-1],
        padded[1:-1, 1:-1, 2:],
        padded[1:-1, 1:-1, :-2],
    ]


def operate(values, padded, conduct):
    summed = jnp.zeros_like(values)
    for face_k, beside in zip(conduct, neighbours(padded)):
        summed = summed + face_k * (values - beside)
    return summed


def kappa_of(indices, length):
    return 4.0 * jnp.sin(jnp.pi * indices / length) ** 2


def pad_sides(padded):
    return jnp.pad(padded, ((0, 0), (1, 1), (1, 1)))


def with_faces(values):
    return pad_sides(with_halo(values, (("space", 0),), 1))


def squares(residual):
    return lax.psum(jnp.sum(residual * residual), "space")


def hartley(length):
    indices = jnp.arange(length, dtype=jnp.int32)
    products = indices[:, None] * indices[None, :] % length
    angles = products.astype(jnp.float32) * (2.0 * jnp.pi / length)
    return jnp.cos(angles) + jnp.sin(angles)


def on_device(log_k, heads, warm_adjoint, obs_columns, obs_residuals, well_columns):
    slab_rows, width_cells, depth_cells = log_k.shape
    space_count = lax.axis_size("space")
    first_row = lax.axis_index("space") * slab_rows
    logk_pad, head_pad = (
        with_halo(log_k, (("space", 0),), 1),
        with_halo(heads[0], (("space", 0),), 1),
    )
    logk_val = log_k.astype(jnp.float32)
    conduct = [
        jnp.exp(0.5 * (logk_val + beside))
        for beside in neighbours(pad_sides(logk_pad.astype(jnp.float32)))
    ]
    columns = obs_columns[0]
    row_local = columns // width_cells - first_row
    inside = (row_local >= 0) & (row_local < slab_rows)
    row_local = jnp.where(inside, row_local, slab_rows)
    source = jnp.zeros((slab_rows, width_cells, depth_cells), jnp.float32)
    source = source.at[row_local, columns % width_cells].add(obs_residuals[0], mode="drop")
    adjoint = warm_adjoint[0].astype(jnp.float32)
    lam_padded = with_faces(adjoint)
    residual = source - operate(adjoint, lam_padded, conduct)
    direction = residual
    norm_now = squares(residual)
    for iteration in range(ITERS):
        dir_padded = with_faces(direction)
        applied = operate(direction, dir_padded, conduct)
        step_length = norm_now / lax.psum(jnp.sum(direction * applied), "space")
        adjoint = adjoint + step_length * direction
        lam_padded = lam_padded + step_length * dir_padded
        if iteration + 1 < ITERS:
            residual = residual - step_length * applied
            norm_next = squares(residual)
            direction = residual + norm_next / norm_now * direction
            norm_now = norm_next
    lam_full = pad_sides(with_halo(adjoint, (("space", 0),), 1))
    head_val = heads[0].astype(jnp.float32)
    misfit_term = jnp.zeros_like(adjoint)
    for face_k, lam_side, head_side in zip(
        conduct, neighbours(lam_full), neighbours(pad_sides(head_pad.astype(jnp.float32)))
    ):
        misfit_term = misfit_term + face_k * (adjoint - lam_side) * (head_val - head_side)
    column_ids = (first_row + jnp.arange(slab_rows, dtype=jnp.int32))[
        :, None
    ] * width_cells + jnp.arange(width_cells, dtype=jnp.int32)[None, :]
    keep_mask = (column_ids != well_columns[0]).astype(jnp.float32)
    partial_value = -0.5 * misfit_term * keep_mask[:, :, None]
    highest = lax.Precision.HIGHEST
    cas_depth = hartley(depth_cells)
    cas_across = hartley(width_cells)
    along_cells = slab_rows * space_count
    cas_along = hartley(along_cells)
    summed = lax.psum_scatter(partial_value, "test", scatter_dimension=1, tiled=True)
    depth_freq = jnp.einsum("xyz,zk->xky", summed, cas_depth, precision=highest)
    pencil = lax.all_to_all(depth_freq, "test", split_axis=1, concat_axis=2, tiled=True)
    across_freq = jnp.einsum("xzy,yk->kzx", pencil, cas_across, precision=highest)
    column_block = lax.all_to_all(across_freq, "space", split_axis=0, concat_axis=2, tiled=True)
    along_freq = jnp.einsum("yzx,xk->yzk", column_block, cas_along, precision=highest)
    across_rows = column_block.shape[0]
    depth_rows = column_block.shape[1]
    kappa_x = kappa_of(jnp.arange(along_cells).astype(jnp.float32), along_cells)
    kappa_y = kappa_of(
        (lax.axis_index("space") * across_rows + jnp.arange(across_rows)).astype(jnp.float32),
        width_cells,
    )
    kappa_z = kappa_of(
        (lax.axis_index("test") * depth_rows + jnp.arange(depth_rows)).astype(jnp.float32),
        depth_cells,
    )
    spectrum = (
        prior_gain
        / (
            1.0
            + range_squared
            * (kappa_y[:, None, None] + kappa_z[None, :, None] + kappa_x[None, None, :])
        )
        ** 2
    )
    along_back = jnp.einsum("yzk,kx->yzx", along_freq * spectrum, cas_along, precision=highest)
    slab_block = lax.all_to_all(along_back, "space", split_axis=2, concat_axis=0, tiled=True)
    across_back = jnp.einsum("yzx,yk->xzk", slab_block, cas_across, precision=highest)
    depth_block = lax.all_to_all(across_back, "test", split_axis=2, concat_axis=1, tiled=True)
    result = jnp.einsum("xky,kz->xyz", depth_block, cas_depth, precision=highest)
    scale_back = 1.0 / (along_cells * width_cells * depth_cells)
    return result * scale_back


def solution(mesh):
    placed = (
        P(("groups", "space"), None, None),
        P("test", ("groups", "space"), None, None),
        P("test", ("groups", "space"), None, None),
        P("test", "groups"),
        P("test", "groups", None),
        P(("groups", "test")),
    )
    return jax.shard_map(
        on_device,
        mesh=mesh,
        in_specs=placed,
        out_specs=P(("groups", "space"), "test", None),
        check_vma=False,
    )
```

profile of v0, /device:TPU:0, one launch (start us, length us, event | category | flops | bytes accessed | tf_op | source)
XLA Modules:
  0.0 745.9 jit_solution(16803509805105050348)
XLA Ops:
  6.5 6.0 fusion.156
  13.3 1.3 collective-permute-start.2
  14.6 6.2 collective-permute-start.3
  21.4 3.9 collective-permute-start
  25.3 1.3 collective-permute-start.1
  26.7 3.8 broadcast_in_dim.4
  30.4 8.1 %scatter_fusion = f32[48,288,128]{2,1,0:T(8,128)} fusion(f32[48,288,128]{2,1,0:T(8,128)} %broadcast_in_dim.4, s32[64]{0:T(128)S(1)} %fusion.127, f32[64,128]{1,0:T(8,128)} %bitcast.94), kind=kCustom, calls=%fused_computation | custom fusion | flops 8192 | bytes 98816 | tf_op jit(solution)/shard_map/scatter-add | solution.py:89
  38.6 1.5 maximum_convert_fusion
  40.1 15.6 %select_maximum_fusion.6 = f32[50,290,130]{2,1,0:T(8,128)} fusion(f32[1,288,128]{2,1,0:T(8,128)} %collective-permute-done.2, f32[48,288,128]{2,1,0:T(8,128)} %get-tuple-element.21, f32[1,288,128]{2,1,0:T(8,128)} %collective-permute-done.3), kind=kLoop, calls=%fused_computation.31 | loop fusion | flops 28275000 | bytes 14912800 | tf_op jit(solution)/shard_map/concatenate | solution.py:19
  55.7 39.1 %fusion.65 = f32[48,288,128]{2,1,0:T(8,128)} fusion(f32[48,288,128]{2,1,0:T(8,128)} %scatter_fusion, f32[48,288,128]{2,1,0:T(8,128)} %get-tuple-element.21, f32[50,290,130]{2,1,0:T(8,128)} %select_maximum_fusion.6, f32[1,288,128]{2,1,0:T(8,128)} %collective-permute-done.3, f32[1,288,128]{2,1,0:T(8,128)} %collective-permute-done.2, ...), kind=kLoop, calls=%fused_computation.117 | loop fusion | flops 58392576 | bytes 74907648 | tf_op jit(solution)/shard_map/sub | solution.py:92
  94.8 1.0 fusion.154
  95.8 1.3 collective-permute-start.4
  97.1 5.7 collective-permute-start.5
  103.5 1.5 collective-permute-done.5
  104.9 13.9 %select_maximum_fusion.4 = f32[50,290,130]{2,1,0:T(8,128)} fusion(f32[1,288,128]{2,1,0:T(8,128)S(1)} %collective-permute-done.4, f32[48,288,128]{2,1,0:T(8,128)} %fusion.65, f32[1,288,128]{2,1,0:T(8,128)S(1)} %collective-permute-done.5), kind=kLoop, calls=%fused_computation.29 | loop fusion | flops 28275000 | bytes 14912800 | tf_op jit(solution)/shard_map/concatenate | solution.py:19
  118.9 36.6 %multiply_reduce_fusion.1 = (f32[]{:T(128)}, f32[]{:T(128)}, f32[48,288,128]{2,1,0:T(8,128)}) fusion(f32[48,288,128]{2,1,0:T(8,128)} %fusion.65, f32[50,290,130]{2,1,0:T(8,128)} %select_maximum_fusion.4, f32[50,288,128]{2,1,0:T(8,128)S(1)} %maximum_convert_fusion, f32[1,288,128]{2,1,0:T(8,128)S(1)} %collective-permute-done.5, ...), kind=kLoop, calls=%fused_computation.138 | loop fusion | flops 63700992 | bytes 67829768 | tf_op jit(solution)/shard_map/reduce_sum | solution.py:98
  155.4 14.1 %all-reduce.6 = (f32[]{:T(128)}, f32[]{:T(128)}) all-reduce(f32[]{:T(128)} %get-tuple-element.6, f32[]{:T(128)} %get-tuple-element.5), channel_id=1, replica_groups=mesh['groups'=2,'space'=4,'test'=4] {'space'}, use_global_device_ids=true, to_apply=%region_2.3 | all-reduce | flops 2 | bytes 16 | tf_op jit(solution)/shard_map/psum | solution.py:61
  170.9 7.4 multiply_reduce_fusion
  178.4 9.0 %psum.30 = f32[]{:T(128)} all-reduce(f32[]{:T(128)} %multiply_reduce_fusion), channel_id=1, replica_groups=mesh['groups'=2,'space'=4,'test'=4] {'space'}, use_global_device_ids=true, to_apply=%region_6.7 | all-reduce | flops 1 | bytes 8 | tf_op jit(solution)/shard_map/psum | solution.py:61
  188.7 6.4 multiply_add_fusion.1
  195.2 1.3 collective-permute-start.6
  196.5 4.6 collective-permute-start.7
  201.1 1.6 slice_bitcast_fusion.3
  202.7 1.3 collective-permute-start.10
  204.0 5.3 collective-permute-start.9
  211.3 10.4 %select_maximum_fusion.2 = f32[50,290,130]{2,1,0:T(8,128)} fusion(f32[1,288,128]{2,1,0:T(8,128)S(1)} %collective-permute-done.6, f32[48,288,128]{2,1,0:T(8,128)S(1)} %multiply_add_fusion.1, f32[1,288,128]{2,1,0:T(8,128)S(1)} %collective-permute-done.7), kind=kLoop, calls=%fused_computation.27 | loop fusion | flops 28275000 | bytes 14912800 | tf_op jit(solution)/shard_map/concatenate | solution.py:19
  221.7 51.6 %fusion.38 = f32[]{:T(128)} fusion(f32[48,288,128]{2,1,0:T(8,128)} %copy-done.3, f32[50,290,130]{2,1,0:T(8,128)} %select_maximum_fusion.2, f32[1,288,128]{2,1,0:T(8,128)} %copy-done.7, f32[1,288,128]{2,1,0:T(8,128)} %copy-done.5, f32[50,288,128]{2,1,0:T(8,128)} %copy-done, bf16[48,288,128]{2,1,0:T(8,128)(2,1)S(1)} %copy-done.1), kind=kLoop, calls=%fused_computation.78 | loop fusion | flops 60162048 | bytes 60751876 | tf_op jit(solution)/shard_map/reduce_sum | solution.py:98
  274.0 10.3 %psum.31 = f32[]{:T(128)} all-reduce(f32[]{:T(128)} %fusion.38), channel_id=1, replica_groups=mesh['groups'=2,'space'=4,'test'=4] {'space'}, use_global_device_ids=true, to_apply=%region_8.9 | all-reduce | flops 1 | bytes 8 | tf_op jit(solution)/shard_map/psum | solution.py:98
  285.7 7.3 multiply_add_fusion
  293.0 2.5 collective-permute-start.11
  295.5 1.5 collective-permute-start.8
  297.1 4.4 maximum_convert_fusion.1
  301.5 1.0 collective-permute-done.8
  303.2 10.4 %select_maximum_fusion = f32[50,290,130]{2,1,0:T(8,128)} fusion(f32[1,288,128]{2,1,0:T(8,128)S(1)} %collective-permute-done.8, f32[48,288,128]{2,1,0:T(8,128)S(1)} %multiply_add_fusion, f32[1,288,128]{2,1,0:T(8,128)S(1)} %collective-permute-done.11), kind=kLoop, calls=%fused_computation.25 | loop fusion | flops 28275000 | bytes 14912800 | tf_op jit(solution)/shard_map/concatenate | solution.py:19
  313.6 70.3 %fusion.21 = f32[48,288,128]{2,1,0:T(8,128)} fusion(f32[50,288,128]{2,1,0:T(8,128)} %maximum_convert_fusion.1, f32[48,288,128]{2,1,0:T(8,128)} %copy-done.2, f32[50,290,130]{2,1,0:T(8,128)} %select_maximum_fusion, f32[1,288,128]{2,1,0:T(8,128)} %copy-done.6, f32[1,288,128]{2,1,0:T(8,128)} %copy-done.8, f32[48,288]{1,0:T(8,128)} %fusion.116, ...), kind=kLoop, calls=%fused_computation.54 | loop fusion | flops 81395712 | bytes 92971008 | tf_op jit(solution)/shard_map/mul | solution.py:117
  384.0 63.7 %reduce-scatter.2.cloned.1.call-done = f32[48,72,128]{2,1,0:T(8,128)} async-done(((f32[48,288,128]{2,1,0:T(8,128)}), f32[48,72,128]{2,1,0:T(8,128)}) %reduce-scatter.2.cloned.1.call-update) | async-done | bytes 1769488 | tf_op jit(solution)/shard_map/reduce_scatter | solution.py:123
  447.7 4.5 convolution_bitcast_fusion.1
  452.2 2.3 copy.29
  454.5 39.9 %all_to_all.72 = f32[48,128,72]{2,0,1:T(8,128)S(1)} all-to-all(f32[48,128,72]{2,0,1:T(8,128)S(1)} %copy.29), channel_id=1, replica_groups=mesh['groups'=2,'space'=4,'test'=4] {'test'}, dimensions={1} | all-to-all | bytes 3538944 | tf_op jit(solution)/shard_map/all_to_all | solution.py:125
  494.4 2.0 copy.31
  496.4 2.6 all_to_all.55
  499.0 7.8 %convolution_bitcast_fusion = f32[288,32,48]{0,2,1:T(8,128)S(1)} fusion(f32[48,32,288]{2,0,1:T(8,128)} %all_to_all.55), kind=kOutput, calls=%fused_computation.150 | convolution fusion | flops 1529653248 | bytes 3538944 | tf_op jit(solution)/shard_map/xzy,yk->kzx/dot_general | solution.py:126
  506.8 5.5 copy.32
  512.3 6.9 reshape.202
  519.2 4.8 all-to-all-start.1
  524.8 39.9 %all-to-all-done.1 = f32[4,1,110592]{2,1,0:T(1,128)S(1)} async-done(((f32[4,1,110592]{2,1,0:T(1,128)}), f32[4,1,110592]{2,1,0:T(1,128)S(1)}, u32[]{:S(2)}, u32[]{:S(2)}) %all-to-all-start.1) | async-done | bytes 1769504 | tf_op jit(solution)/shard_map/all_to_all | solution.py:127
  565.3 5.8 reduce
  571.1 4.3 reshape.203
  575.4 3.8 copy.33
  579.2 3.0 copy.34
  582.2 4.5 fusion.105
  586.8 4.6 fusion.77
  591.4 3.7 copy.35
  595.1 73.1 %all_to_all.73 = f32[72,32,192]{0,1,2:T(8,128)S(1)} all-to-all(f32[72,32,192]{0,1,2:T(8,128)S(1)} %copy.35), channel_id=1, replica_groups=mesh['groups'=2,'space'=4,'test'=4] {'space'}, dimensions={2} | all-to-all | bytes 3538944 | tf_op jit(solution)/shard_map/all_to_all | solution.py:150
  668.2 2.0 copy.37
  670.2 2.6 reshape.199
  672.8 7.8 %fusion.95 = f32[288,1536]{0,1:S(1)} fusion(f32[288,1536]{0,1:T(8,128)} %reshape.199), kind=kOutput, calls=%fused_computation.168 | convolution fusion | flops 1529653248 | bytes 3538944
  680.6 5.5 copy.38
  686.1 5.9 reshape.204
  692.0 24.8 %all_to_all.74 = f32[4,1,110592]{2,1,0:T(1,128)S(1)} all-to-all(f32[4,1,110592]{2,1,0:T(1,128)S(1)} %reshape.204), channel_id=1, replica_groups=mesh['groups'=2,'space'=4,'test'=4] {'test'}, dimensions={0} | all-to-all | bytes 3538944 | tf_op jit(solution)/shard_map/all_to_all | solution.py:152
  716.8 5.8 reduce.1
  722.6 4.3 reshape.205
  726.9 5.5 copy.39
  732.5 6.3 convolution_multiply_fusion
  (46 shorter events, 6.2 us)
Async XLA Ops:
  6.5 14.2 %copy-start.1 = (bf16[48,288,128]{2,1,0:T(8,128)(2,1)S(1)}, bf16[48,288,128]{2,1,0:T(8,128)(2,1)}, u32[]{:S(2)}) copy-start(bf16[48,288,128]{2,1,0:T(8,128)(2,1)} %param.6) | copy-start | bytes 10616836
  6.5 20.1 %copy-start.10 = (s32[1,64]{1,0:T(1,128)S(1)}, s32[1,64]{1,0:T(1,128)}, u32[]{:S(2)}) copy-start(s32[1,64]{1,0:T(1,128)} %param.9) | copy-start | bytes 772
  6.5 441.1 %reduce-scatter.2.cloned.1.call-start = ((), (), s32[]{:S(2)}) async-start(), calls=%async_computation.5 | async-start | bytes 8847360 | tf_op jit(solution)/shard_map/reduce_scatter | solution.py:123
  13.3 26.8 %collective-permute-start.2 = (f32[1,288,128]{2,1,0:T(8,128)}, f32[1,288,128]{2,1,0:T(8,128)}, u32[]{:S(2)}, u32[]{:S(2)}) collective-permute-start(f32[1,288,128]{2,1,0:T(8,128)} %get-tuple-element.17), channel_id=1, source_target_pairs={{4,0},{8,4},{12,8},{5,1},{9,5},{13,9},{6,2},{10,6},{14,10},{7,3},{... | collective-permute-start | bytes 442376 | tf_op jit(solution)/shard_map/ppermute | solution.py:23
  14.6 25.5 %collective-permute-start.3 = (f32[1,288,128]{2,1,0:T(8,128)}, f32[1,288,128]{2,1,0:T(8,128)}, u32[]{:S(2)}, u32[]{:S(2)}) collective-permute-start(f32[1,288,128]{2,1,0:T(8,128)} %get-tuple-element.16), channel_id=1, source_target_pairs={{0,4},{4,8},{8,12},{1,5},{5,9},{9,13},{2,6},{6,10},{10,14},{3,7},{... | collective-permute-start | bytes 442376 | tf_op jit(solution)/shard_map/ppermute | solution.py:21
  21.4 17.1 %collective-permute-start = (bf16[1,288,128]{2,1,0:T(8,128)(2,1)}, bf16[1,288,128]{2,1,0:T(8,128)(2,1)}, u32[]{:S(2)}, u32[]{:S(2)}) collective-permute-start(bf16[1,288,128]{2,1,0:T(8,128)(2,1)} %get-tuple-element.18), channel_id=1, source_target_pairs={{0,4},{4,8},{8,12},{1,5},{5,9},{9,13},{2,6},{6,10},{10,14},{3,7},{... | collective-permute-start | bytes 221192 | tf_op jit(solution)/shard_map/ppermute | solution.py:21
  25.3 13.2 %collective-permute-start.1 = (bf16[1,288,128]{2,1,0:T(8,128)(2,1)}, bf16[1,288,128]{2,1,0:T(8,128)(2,1)}, u32[]{:S(2)}, u32[]{:S(2)}) collective-permute-start(bf16[1,288,128]{2,1,0:T(8,128)(2,1)} %get-tuple-element.19), channel_id=1, source_target_pairs={{4,0},{8,4},{12,8},{5,1},{9,5},{13,9},{6,2},{10,6},{14,10},{7,3},{... | collective-permute-start | bytes 221192 | tf_op jit(solution)/shard_map/ppermute | solution.py:23
  40.1 78.8 %copy-start = (f32[50,288,128]{2,1,0:T(8,128)}, f32[50,288,128]{2,1,0:T(8,128)S(1)}, u32[]{:S(2)}) copy-start(f32[50,288,128]{2,1,0:T(8,128)S(1)} %maximum_convert_fusion) | copy-start | bytes 22118404
  95.8 7.7 %collective-permute-start.4 = (f32[1,288,128]{2,1,0:T(8,128)S(1)}, f32[1,288,128]{2,1,0:T(8,128)S(1)}, u32[]{:S(2)}, u32[]{:S(2)}) collective-permute-start(f32[1,288,128]{2,1,0:T(8,128)S(1)} %get-tuple-element.15), channel_id=1, source_target_pairs={{4,0},{8,4},{12,8},{5,1},{9,5},{13,9},{6,2},{10,6},{14,10},{7,3},{... | collective-permute-start | bytes 442376 | tf_op jit(solution)/shard_map/ppermute | solution.py:23
  97.1 7.8 %collective-permute-start.5 = (f32[1,288,128]{2,1,0:T(8,128)S(1)}, f32[1,288,128]{2,1,0:T(8,128)S(1)}, u32[]{:S(2)}, u32[]{:S(2)}) collective-permute-start(f32[1,288,128]{2,1,0:T(8,128)S(1)} %get-tuple-element.14), channel_id=1, source_target_pairs={{0,4},{4,8},{8,12},{1,5},{5,9},{9,13},{2,6},{6,10},{10,14},{3,7},{... | collective-permute-start | bytes 442376 | tf_op jit(solution)/shard_map/ppermute | solution.py:21
  195.2 14.8 %copy-start.3 = (f32[48,288,128]{2,1,0:T(8,128)}, f32[48,288,128]{2,1,0:T(8,128)S(1)}, u32[]{:S(2)}) copy-start(f32[48,288,128]{2,1,0:T(8,128)S(1)} %multiply_add_fusion.1) | copy-start | bytes 21233668
  195.2 14.7 %collective-permute-start.6 = (f32[1,288,128]{2,1,0:T(8,128)S(1)}, f32[1,288,128]{2,1,0:T(8,128)S(1)}, u32[]{:S(2)}, u32[]{:S(2)}) collective-permute-start(f32[1,288,128]{2,1,0:T(8,128)S(1)} %get-tuple-element.13), channel_id=1, source_target_pairs={{4,0},{8,4},{12,8},{5,1},{9,5},{13,9},{6,2},{10,6},{14,10},{7,3},{... | collective-permute-start | bytes 442376 | tf_op jit(solution)/shard_map/ppermute | solution.py:23
  196.5 13.5 %collective-permute-start.7 = (f32[1,288,128]{2,1,0:T(8,128)S(1)}, f32[1,288,128]{2,1,0:T(8,128)S(1)}, u32[]{:S(2)}, u32[]{:S(2)}) collective-permute-start(f32[1,288,128]{2,1,0:T(8,128)S(1)} %get-tuple-element.12), channel_id=1, source_target_pairs={{0,4},{4,8},{8,12},{1,5},{5,9},{9,13},{2,6},{6,10},{10,14},{3,7},{... | collective-permute-start | bytes 442376 | tf_op jit(solution)/shard_map/ppermute | solution.py:21
  202.7 94.4 %collective-permute-start.10 = (bf16[1,288,128]{2,1,0:T(8,128)(2,1)}, bf16[1,288,128]{2,1,0:T(8,128)(2,1)}, u32[]{:S(2)}, u32[]{:S(2)}) collective-permute-start(bf16[1,288,128]{2,1,0:T(8,128)(2,1)} %get-tuple-element.23), channel_id=1, source_target_pairs={{4,0},{8,4},{12,8},{5,1},{9,5},{13,9},{6,2},{10,6},{14,10},{7,3},{... | collective-permute-start | bytes 221192 | tf_op jit(solution)/shard_map/ppermute | solution.py:23
  204.0 93.1 %collective-permute-start.9 = (bf16[1,288,128]{2,1,0:T(8,128)(2,1)}, bf16[1,288,128]{2,1,0:T(8,128)(2,1)}, u32[]{:S(2)}, u32[]{:S(2)}) collective-permute-start(bf16[1,288,128]{2,1,0:T(8,128)(2,1)} %get-tuple-element.22), channel_id=1, source_target_pairs={{0,4},{4,8},{8,12},{1,5},{5,9},{9,13},{2,6},{6,10},{10,14},{3,7},{... | collective-permute-start | bytes 221192 | tf_op jit(solution)/shard_map/ppermute | solution.py:21
  210.0 0.7 copy-start.5
  210.6 0.7 copy-start.7
  285.7 11.4 %copy-start.4 = (bf16[1,48,288,128]{3,2,1,0:T(8,128)(2,1)S(1)}, bf16[1,48,288,128]{3,2,1,0:T(8,128)(2,1)}, u32[]{:S(2)}) copy-start(bf16[1,48,288,128]{3,2,1,0:T(8,128)(2,1)} %param.7) | copy-start | bytes 10616836
  292.9 9.6 %copy-start.2 = (f32[48,288,128]{2,1,0:T(8,128)}, f32[48,288,128]{2,1,0:T(8,128)S(1)}, u32[]{:S(2)}) copy-start(f32[48,288,128]{2,1,0:T(8,128)S(1)} %multiply_add_fusion) | copy-start | bytes 21233668
  293.0 8.5 %collective-permute-start.11 = (f32[1,288,128]{2,1,0:T(8,128)S(1)}, f32[1,288,128]{2,1,0:T(8,128)S(1)}, u32[]{:S(2)}, u32[]{:S(2)}) collective-permute-start(f32[1,288,128]{2,1,0:T(8,128)S(1)} %get-tuple-element.10), channel_id=1, source_target_pairs={{0,4},{4,8},{8,12},{1,5},{5,9},{9,13},{2,6},{6,10},{10,14},{3,7},{... | collective-permute-start | bytes 442376 | tf_op jit(solution)/shard_map/ppermute | solution.py:21
  295.5 7.0 collective-permute-start.8
  301.5 1.1 copy-start.6
  302.6 0.7 copy-start.8
  519.2 45.6 %all-to-all-start.1 = ((f32[4,1,110592]{2,1,0:T(1,128)}), f32[4,1,110592]{2,1,0:T(1,128)S(1)}, u32[]{:S(2)}, u32[]{:S(2)}) async-start(f32[4,1,110592]{2,1,0:T(1,128)} %reshape.202), calls=%async_computation.2 | async-start | bytes 3538944 | tf_op jit(solution)/shard_map/all_to_all | solution.py:127
  579.2 7.6 %copy-start.9 = (f32[72,32]{1,0:T(8,128)S(1)}, f32[72,32]{1,0:T(8,128)}, u32[]{:S(2)}) copy-start(f32[72,32]{1,0:T(8,128)} %broadcast_add_fusion) | copy-start | bytes 27652
Sparse Core Ops, SparseCore 0:
  384.1 63.5 reduce-scatter.1
where the time goes:
time: 755 us; the launch traced here: 746 us
  other arithmetic  302 us (40%)
  blocking collectives  171 us (23%)
  waiting for transfers between devices  107 us (14%)
  local copies, waits for them, and re-layouts  70.3 us (9%)
  starting transfers between devices  41 us (5%)
  matrix products  35.6 us (5%)
  between operations  18.7 us (2%)
    reduce_sum x2, other arithmetic, on_device(): step_length = norm_now / lax.psum(jnp.sum(direction * applied), 'space')  88.2 us
    all_to_all x1, blocking collectives, on_device(): lax.all_to_all(along_back, 'space', split_axis=2, concat_axis=0, tiled=True)  73.1 us
    mul x2, other arithmetic, on_device(): partial_value = -0.5 * misfit_term * keep_mask[:, :, None]  71 us
    reduce_scatter x1, waiting for transfers between devices, on_device(): lax.psum_scatter(partial_value, 'test', scatter_dimension=1, tiled=True)  63.7 us
    concatenate x4, other arithmetic, with_halo(): jnp.concatenate([lax.ppermute(tail, axis, [(i, (i + 1) % count) for i in...  50.4 us
    all_to_all x1, waiting for transfers between devices, on_device(): lax.all_to_all(across_freq, 'space', split_axis=0, concat_axis=2, tiled=T...  39.9 us
    all_to_all x1, blocking collectives, on_device(): lax.all_to_all(depth_freq, 'test', split_axis=1, concat_axis=2, tiled=True)  39.9 us
    sub x1, other arithmetic, on_device(): residual = source - operate(adjoint, lam_padded, conduct)  39.1 us
  transfers between devices with their start and end apart: 14, of which 5 were waited for; matrix products, arithmetic and copies ran while one was open for 12% of the time, Pallas kernels for 0%

commit v1 on v0

--- a/solution.py
+++ b/solution.py
@@ -1,6 +1,10 @@
+import functools
+
 import jax
 import jax.numpy as jnp
 from jax import lax
+from jax.experimental import pallas as pl
+from jax.experimental.pallas import tpu as pltpu
 from jax.sharding import PartitionSpec as P
 
 ITERS = 2
@@ -155,6 +159,412 @@
     return result * scale_back
 
 
+HIGHEST = lax.Precision.HIGHEST
+VM = pl.BlockSpec(memory_space=pltpu.VMEM)
+SM = pl.BlockSpec(memory_space=pltpu.SMEM)
+BIG = pltpu.CompilerParams(vmem_limit_bytes=60 * 1024 * 1024)
+
+
+def shape(*dims, dtype=jnp.float32):
+    return jax.ShapeDtypeStruct(dims, dtype)
+
+
+def iotas(plane):
+    return (
+        lax.broadcasted_iota(jnp.int32, plane, 0),
+        lax.broadcasted_iota(jnp.int32, plane, 1),
+    )
+
+
+def ring_sum(plane, edge):
+    rows, lanes = plane.shape
+    at_row, at_lane = iotas(plane.shape)
+    up = jnp.where(at_row == rows - 1, edge, pltpu.roll(plane, rows - 1, 0))
+    down = jnp.where(at_row == 0, edge, pltpu.roll(plane, 1, 0))
+    right = jnp.where(at_lane == lanes - 1, edge, pltpu.roll(plane, lanes - 1, 1))
+    left = jnp.where(at_lane == 0, edge, pltpu.roll(plane, 1, 1))
+    return (up + down) + (right + left)
+
+
+def plane_total(plane):
+    rows, lanes = plane.shape
+    return jnp.sum(plane.reshape(rows // 8, 8, lanes), axis=0)
+
+
+def swap_blocks(planes):
+    count = len(planes)
+    lanes = planes[0].shape[1]
+    block = lanes // count
+    at_lane = iotas(planes[0].shape)[1] // block
+    swapped = []
+    for to in range(count):
+        joined = planes[to]
+        for frm in range(count):
+            if frm != to:
+                shift = (block * (frm - to)) % lanes
+                joined = jnp.where(at_lane == frm, pltpu.roll(planes[frm], shift, 1), joined)
+        swapped.append(joined)
+    return swapped
+
+
+def residual_kernel(
+    spot, columns, logk, warm, before, after, observed, start, image, soft, around, sums, weighted
+):
+    rows, width, depth = logk.shape
+    first_row, last_row = spot[0], spot[1]
+
+    def prepare(to, logk_row, warm_row):
+        soft_row = jnp.exp(0.5 * logk_row.astype(jnp.float32))
+        soft[to] = soft_row
+        weighted[to] = soft_row * warm_row.astype(jnp.float32)
+
+    for i in range(3):
+        prepare(i, before[i], before[3 + i])
+        prepare(rows + 3 + i, after[i], after[3 + i])
+
+    def fill(i, _):
+        prepare(i + 3, logk[i], warm[i])
+        return 0
+
+    lax.fori_loop(0, rows, fill, 0)
+
+    def first(i, _):
+        row = first_row + i - 2
+        inside = ((row >= 0) & (row < last_row)).astype(jnp.float32)
+        soft_row = soft[i + 1]
+        near = ring_sum(soft_row, 1.0) + (soft[i] + soft[i + 2])
+        around[i] = near
+        held = weighted[i + 1]
+        beside = ring_sum(held, 0.0) + (weighted[i] + weighted[i + 2])
+        start[i] = (soft_row * beside - held * near) * inside
+        return 0
+
+    lax.fori_loop(0, rows + 4, first, 0)
+
+    def add(o, _):
+        column = columns[0, o]
+        row = column // width
+        place = column - row * width
+        local = row - first_row + 2
+
+        @pl.when((local >= 0) & (local < rows + 4))
+        def _():
+            start[local, pl.ds(place, 1), :] += observed[pl.ds(o, 1), :]
+
+        return 0
+
+    lax.fori_loop(0, columns.shape[1], add, 0)
+
+    def scale(i, _):
+        weighted[i] = soft[i + 1] * start[i]
+        return 0
+
+    lax.fori_loop(0, rows + 4, scale, 0)
+
+    def second(i, carry):
+        total_rr, total_rq = carry
+        row = first_row + i - 1
+        inside = ((row >= 0) & (row < last_row)).astype(jnp.float32)
+        held = weighted[i + 1]
+        beside = ring_sum(held, 0.0) + (weighted[i] + weighted[i + 2])
+        applied = (held * around[i + 1] - soft[i + 2] * beside) * inside
+        image[i] = applied
+        value = start[i + 1]
+        own = ((i >= 1) & (i <= rows)).astype(jnp.float32)
+        return (
+            total_rr + own * plane_total(value * value),
+            total_rq + own * plane_total(value * applied),
+        )
+
+    zero = jnp.zeros((8, depth), jnp.float32)
+    total_rr, total_rq = lax.fori_loop(0, rows + 2, second, (zero, zero))
+    sums[0] = total_rr
+    sums[1] = total_rq
+
+
+def second_kernel(scalars, start, image, soft, around, sums, weighted):
+    rows = start.shape[0] - 4
+    step = scalars[0]
+
+    def scale(i, _):
+        weighted[i] = soft[i + 2] * (start[i + 1] - step * image[i])
+        return 0
+
+    lax.fori_loop(0, rows + 2, scale, 0)
+
+    def apply(i, carry):
+        total_rr, total_rq = carry
+        held = weighted[i + 1]
+        beside = ring_sum(held, 0.0) + (weighted[i] + weighted[i + 2])
+        value = start[i + 2] - step * image[i + 1]
+        applied = held * around[i + 2] - soft[i + 3] * beside
+        return total_rr + plane_total(value * value), total_rq + plane_total(value * applied)
+
+    zero = jnp.zeros((8, start.shape[2]), jnp.float32)
+    total_rr, total_rq = lax.fori_loop(0, rows, apply, (zero, zero))
+    sums[0] = total_rr
+    sums[1] = total_rq
+
+
+def face_terms(soft, field, head, axis):
+    size = soft.shape[axis]
+    at = iotas(soft.shape)[axis]
+    both = field * head
+    ahead = size - 1
+    product = (field - pltpu.roll(field, ahead, axis)) * (head - pltpu.roll(head, ahead, axis))
+    upper = jnp.where(at == size - 1, both, pltpu.roll(soft, ahead, axis) * product)
+    lower = jnp.where(at == 0, both, pltpu.roll(soft * product, 1, axis))
+    return upper + lower
+
+
+def gradient_kernel(
+    spot, scalars, warm, heads, before, after, start, image, soft, cas, out, field, head
+):
+    rows, width, depth = warm.shape
+    first_row = spot[0]
+    well = spot[2]
+    with_start, with_image = scalars[0], scalars[1]
+
+    def fill(to, warm_row, head_row):
+        field[to] = (
+            warm_row.astype(jnp.float32) + with_start * start[to + 1] - with_image * image[to]
+        )
+        head[to] = head_row.astype(jnp.float32)
+
+    fill(0, before[5], before[6])
+    fill(rows + 1, after[3], after[6])
+
+    def middle(i, _):
+        fill(i + 1, warm[i], heads[i])
+        return 0
+
+    lax.fori_loop(0, rows, middle, 0)
+    at_row = iotas((width, depth))[0]
+    count = out.shape[0]
+
+    def term(i):
+        s, f, h = soft[i + 3], field[i + 1], head[i + 1]
+        gathered = face_terms(s, f, h, 0) + face_terms(s, f, h, 1)
+        gathered += soft[i + 2] * ((f - field[i]) * (h - head[i]))
+        gathered += soft[i + 4] * ((f - field[i + 2]) * (h - head[i + 2]))
+        keep = at_row != well - (first_row + i) * width
+        value = jnp.where(keep, -0.5 * s * gathered, 0.0)
+        return jnp.dot(value, cas[...], precision=HIGHEST, preferred_element_type=jnp.float32)
+
+    def group(g, _):
+        for t, plane in enumerate(swap_blocks([term(g * count + p) for p in range(count)])):
+            out[t, g] = plane
+        return 0
+
+    lax.fori_loop(0, rows // count, group, 0)
+
+
+def moment_kernel(count, summed, cas, rho, freq, moments):
+    groups, width, lanes = summed.shape
+    part = width // count
+
+    def across(g, _):
+        mixed = jnp.dot(cas[...], summed[g], precision=HIGHEST, preferred_element_type=jnp.float32)
+        blocks = [mixed[j * part : (j + 1) * part] for j in range(count)]
+        for p, plane in enumerate(swap_blocks(blocks)):
+            freq[g * count + p] = plane
+        return 0
+
+    lax.fori_loop(0, groups, across, 0)
+    pole = rho[...]
+    rows = groups * count
+
+    def walk(i, carry):
+        one, two, back_one, back_two = carry
+        value, back = freq[i], freq[rows - 1 - i]
+        return (
+            value + pole * one,
+            pole * (two + one),
+            back + pole * back_one,
+            pole * (back_two + back_one),
+        )
+
+    zero = jnp.zeros((part, lanes), jnp.float32)
+    ends = lax.fori_loop(0, rows, walk, (zero, zero, zero, zero))
+    for n in range(4):
+        moments[n] = ends[n]
+
+
+def filter_kernel(count, where_at, freq, moments, tables, cas, out, filtered):
+    rows, part, lanes = freq.shape
+    slabs = moments.shape[0]
+    me = where_at[0]
+    pole, level, slope, decay, wrap_one, wrap_two = (tables[n] for n in range(6))
+
+    def carried(direction, n):
+        one = jnp.zeros((part, lanes), jnp.float32)
+        two = one
+        for m in range(slabs, 0, -1):
+            other = lax.rem(me + 2 * slabs - direction * m, slabs)
+            one, two = (
+                decay * one + moments[other, n],
+                decay * (two + rows * one) + moments[other, n + 1],
+            )
+        return wrap_one * one, wrap_one * two + wrap_two * one
+
+    def forward(i, carry):
+        one, two = carry
+        two = pole * (two + one)
+        one = freq[i] + pole * one
+        filtered[i] = level * one + slope * two
+        return one, two
+
+    lax.fori_loop(0, rows, forward, carried(1, 0))
+
+    def backward(i, carry):
+        one, two = carry
+        at = rows - 1 - i
+        two = pole * (two + one)
+        one = pole * one
+        filtered[at] += level * one + slope * two
+        return one + freq[at], two
+
+    lax.fori_loop(0, rows, backward, carried(-1, 2))
+
+    def across(g, _):
+        blocks = swap_blocks([filtered[g * count + p] for p in range(count)])
+        stacked = jnp.concatenate(blocks, axis=0)
+        mixed = jnp.dot(cas[...], stacked, precision=HIGHEST, preferred_element_type=jnp.float32)
+        for u in range(count):
+            out[u, g] = mixed[u * part : (u + 1) * part]
+        return 0
+
+    lax.fori_loop(0, rows // count, across, 0)
+
+
+def depth_kernel(received, cas, out):
+    count, groups, part, lanes = received.shape
+
+    def back(g, _):
+        for p, plane in enumerate(swap_blocks([received[t, g] for t in range(count)])):
+            out[g * count + p] = jnp.dot(
+                plane, cas[...], precision=HIGHEST, preferred_element_type=jnp.float32
+            )
+        return 0
+
+    lax.fori_loop(0, groups, back, 0)
+
+
+def space_sum(sums):
+    both = lax.psum(jnp.sum(sums, axis=(1, 2)), "space")
+    return both[0], both[1]
+
+
+def fast(log_k, heads, warm_adjoint, obs_columns, obs_residuals, well_columns):
+    rows, width, depth = log_k.shape
+    slabs = lax.axis_size("space")
+    count = lax.axis_size("test")
+    along = rows * slabs
+    part = width // count
+    block = depth // count
+    first_row = lax.axis_index("space") * rows
+    warm, head = warm_adjoint[0], heads[0]
+    low = jnp.concatenate([log_k[:3], warm[:3], head[:1]])
+    high = jnp.concatenate([log_k[rows - 3 :], warm[rows - 3 :], head[rows - 1 :]])
+    before = lax.ppermute(high, "space", [(i, i + 1) for i in range(slabs - 1)])
+    after = lax.ppermute(low, "space", [(i + 1, i) for i in range(slabs - 1)])
+    spot = jnp.stack([first_row, jnp.int32(along), well_columns[0]]).astype(jnp.int32)
+    start, image, soft, around, sums = pl.pallas_call(
+        residual_kernel,
+        out_shape=[
+            shape(rows + 4, width, depth),
+            shape(rows + 2, width, depth),
+            shape(rows + 6, width, depth),
+            shape(rows + 4, width, depth),
+            shape(2, 8, depth),
+        ],
+        in_specs=[SM, SM, VM, VM, VM, VM, VM],
+        out_specs=[VM] * 5,
+        scratch_shapes=[pltpu.VMEM((rows + 6, width, depth), jnp.float32)],
+        compiler_params=BIG,
+        name="residual",
+    )(spot, obs_columns, log_k, warm, before, after, obs_residuals[0])
+    norm, curve = space_sum(sums)
+    step = norm / curve
+    sums = pl.pallas_call(
+        second_kernel,
+        out_shape=shape(2, 8, depth),
+        in_specs=[SM, VM, VM, VM, VM],
+        out_specs=VM,
+        scratch_shapes=[pltpu.VMEM((rows + 2, width, depth), jnp.float32)],
+        compiler_params=BIG,
+        name="second",
+    )(step[None], start, image, soft, around)
+    norm_next, curve_next = space_sum(sums)
+    ratio = norm_next / norm
+    step_next = norm_next / (curve_next - ratio * norm_next / step)
+    scalars = jnp.stack([step + step_next * (1.0 + ratio), step_next * step])
+    cas_depth = hartley(depth)
+    cas_across = hartley(width)
+    sent = pl.pallas_call(
+        gradient_kernel,
+        out_shape=shape(count, rows // count, width, depth),
+        in_specs=[SM, SM] + [VM] * 8,
+        out_specs=VM,
+        scratch_shapes=[pltpu.VMEM((rows + 2, width, depth), jnp.float32)] * 2,
+        compiler_params=BIG,
+        name="gradient",
+    )(spot, scalars, warm, head, before, after, start, image, soft, cas_depth)
+    summed = lax.psum_scatter(sent, "test", scatter_dimension=0)
+    lanes_at = jnp.arange(depth)
+    across_at = (lanes_at // block)[None, :] * part + jnp.arange(part)[:, None]
+    depth_at = lax.axis_index("test") * block + lanes_at % block
+    shift = 1.0 + range_squared * (
+        kappa_of(across_at.astype(jnp.float32), width)
+        + kappa_of(depth_at.astype(jnp.float32), depth)[None, :]
+    )
+    centre = 1.0 + shift / (2.0 * range_squared)
+    pole = 1.0 / (centre + jnp.sqrt(centre * centre - 1.0))
+    square = pole * pole
+    gain = prior_gain / (range_squared * range_squared) * square / (width * depth)
+    slope = gain / (1.0 - square) ** 2
+    level = slope * (1.0 + square) / (1.0 - square)
+    turn = pole**along
+    wrap_one = 1.0 / (1.0 - turn)
+    tables = jnp.stack(
+        [pole, level, slope, pole**rows, wrap_one, along * turn * wrap_one * wrap_one]
+    )
+    freq, moments = pl.pallas_call(
+        functools.partial(moment_kernel, count),
+        out_shape=[shape(rows, part, depth), shape(4, part, depth)],
+        in_specs=[VM] * 3,
+        out_specs=[VM] * 2,
+        compiler_params=BIG,
+        name="moment",
+    )(summed, cas_across, pole)
+    moments = lax.all_gather(moments, "space")
+    back = pl.pallas_call(
+        functools.partial(filter_kernel, count),
+        out_shape=shape(count, rows // count, part, depth),
+        in_specs=[SM] + [VM] * 4,
+        out_specs=VM,
+        scratch_shapes=[pltpu.VMEM((rows, part, depth), jnp.float32)],
+        compiler_params=BIG,
+        name="filter",
+    )(lax.axis_index("space").astype(jnp.int32)[None], freq, moments, tables, cas_across)
+    received = lax.all_to_all(back, "test", split_axis=0, concat_axis=0, tiled=True)
+    return pl.pallas_call(
+        depth_kernel,
+        out_shape=shape(rows, part, depth),
+        in_specs=[VM] * 2,
+        out_specs=VM,
+        compiler_params=BIG,
+        name="depth",
+    )(received, cas_depth)
+
+
+def pick(log_k, *rest):
+    rows, width, depth = log_k.shape
+    count = lax.axis_size("test")
+    fits = depth == 128 and depth % count == 0 and rows % count == 0 and width % (8 * count) == 0
+    return (fast if fits and rows >= 3 else on_device)(log_k, *rest)
+
+
 def solution(mesh):
     placed = (
         P(("groups", "space"), None, None),
@@ -165,7 +575,7 @@
         P(("groups", "test")),
     )
     return jax.shard_map(
-        on_device,
+        pick,
         mesh=mesh,
         in_specs=placed,
         out_specs=P(("groups", "space"), "test", None),

time: 755 us -> 302 us (0.40); the launches traced: 746 us -> 301 us
  other arithmetic: 302 us -> 8.49 us
  Pallas kernels: 0 us -> 126 us
  blocking collectives: 171 us -> 64.5 us
  local copies, waits for them, and re-layouts: 70.3 us -> 5.18 us
  waiting for transfers between devices: 107 us -> 70.7 us
  matrix products: 35.6 us -> 0 us
  starting transfers between devices: 41 us -> 6.25 us
    pallas_call x0 -> x6, Pallas kernels: none -> 126 us  [the longest x1 37.3 us: fast(): pl.pallas_call(residual_kernel, out_shape=[shape(rows + 4, width, depth),...]
    all_to_all x3 -> x1, blocking collectives: 138 us -> 26.6 us  [fast(): lax.all_to_all(back, 'test', split_axis=0, concat_axis=0, tiled=True)]
    reduce_sum x3 -> x2, other arithmetic: 95.6 us -> 1.58 us  [space_sum(): both = lax.psum(jnp.sum(sums, axis=(1, 2)), 'space')]
    mul x3 -> x1, other arithmetic: 71 us -> 0.01 us  [fast(): across_at = (lanes_at // block)[None, :] * part + jnp.arange(part)[:, None]]
    concatenate x5 -> x2, other arithmetic: 50.4 us -> 0.13 us  [the longest x1 0.07 us: fast(): high = jnp.concatenate([log_k[rows - 3:], warm[rows - 3:], head[rows - 1:]])]
    all_to_all x1 -> x0, waiting for transfers between devices: 39.9 us -> none  [on_device(): lax.all_to_all(across_freq, 'space', split_axis=0, concat_axis=2, tiled=T...]
    sub x1 -> x0, other arithmetic: 39.1 us -> none  [on_device(): residual = source - operate(adjoint, lam_padded, conduct)]
    ppermute x12 -> x2, starting transfers between devices: 36.2 us -> 6.25 us  [the longest x1 4.96 us: fast(): before = lax.ppermute(high, 'space', [(i, i + 1) for i in range(slabs - 1)])]
  transfers between devices with their start and end apart: 14 -> 3, of which waited for: 5 -> 3; matrix products, arithmetic and copies ran while one was open for 12% -> 2% of each run, Pallas kernels for 0% -> 0%
where the time goes in v1:
time: 302 us; the launch traced here: 301 us
  Pallas kernels  126 us (42%)
  waiting for transfers between devices  70.7 us (23%)
  blocking collectives  64.5 us (21%)
  between operations  20.2 us (7%)
  other arithmetic  8.49 us (3%)
  starting transfers between devices  6.25 us (2%)
  local copies, waits for them, and re-layouts  5.18 us (2%)
    reduce_scatter x1, waiting for transfers between devices, fast(): summed = lax.psum_scatter(sent, 'test', scatter_dimension=0)  58.1 us
    pallas_call x1, Pallas kernels, fast(): pl.pallas_call(residual_kernel, out_shape=[shape(rows + 4, width, depth),...  37.3 us
    pallas_call x1, Pallas kernels, fast(): pl.pallas_call(gradient_kernel, out_shape=shape(count, rows // count, wid...  37.1 us
    all_to_all x1, blocking collectives, fast(): lax.all_to_all(back, 'test', split_axis=0, concat_axis=0, tiled=True)  26.6 us
    all_gather x1, blocking collectives, fast(): moments = lax.all_gather(moments, 'space')  19 us
    pallas_call x1, Pallas kernels, fast(): pl.pallas_call(second_kernel, out_shape=shape(2, 8, depth), in_specs=[SM,...  19 us
    psum x2, blocking collectives, space_sum(): both = lax.psum(jnp.sum(sums, axis=(1, 2)), 'space')  18.9 us
    pallas_call x1, Pallas kernels, fast(): pl.pallas_call(functools.partial(filter_kernel, count), out_shape=shape(c...  12.3 us
  transfers between devices with their start and end apart: 3, of which 3 were waited for; matrix products, arithmetic and copies ran while one was open for 2% of the time, Pallas kernels for 0%

profile of v1, /device:TPU:0, one launch (start us, length us, event | category | flops | bytes accessed | tf_op | source)
XLA Modules:
  0.0 301.0 jit_solution(17119395854466752631)
XLA Ops:
  6.5 0.0 reduce-scatter.2.cloned.1.call-start
  6.5 1.1 fusion.23
  7.6 1.1 slice_bitcast_fusion
  8.7 0.9 slice_bitcast_fusion.2
  9.6 0.1 pad_maximum_fusion
  9.7 5.0 %collective-permute-start = (bf16[7,288,128]{2,1,0:T(8,128)(2,1)S(1)}, bf16[7,288,128]{2,1,0:T(8,128)(2,1)S(1)}, u32[]{:S(2)}, u32[]{:S(2)}) collective-permute-start(bf16[7,288,128]{2,1,0:T(8,128)(2,1)S(1)} %pad_maximum_fusion), channel_id=1, source_target_pairs={{0,4},{4,8},{8,12},{1,5},{5,9},{9,13},{2,6},{6,10},{10,14},{3,7},{... | collective-permute-start | bytes 1548296 | tf_op jit(solution)/shard_map/ppermute | solution.py:469
  14.7 0.1 pad_maximum_fusion.1
  14.7 1.3 collective-permute-start.1
  16.7 0.6 pad_add_fusion.spot
  17.3 8.3 %collective-permute-done.before = bf16[7,288,128]{2,1,0:T(8,128)(2,1)S(1)} collective-permute-done((bf16[7,288,128]{2,1,0:T(8,128)(2,1)S(1)}, bf16[7,288,128]{2,1,0:T(8,128)(2,1)S(1)}, u32[]{:S(2)}, u32[]{:S(2)}) %collective-permute-start) | collective-permute-done | bytes 516128 | tf_op jit(solution)/shard_map/ppermute | solution.py:469
  25.6 0.0 copy-start
  25.6 4.2 %collective-permute-done.1.after = bf16[7,288,128]{2,1,0:T(8,128)(2,1)S(1)} collective-permute-done((bf16[7,288,128]{2,1,0:T(8,128)(2,1)S(1)}, bf16[7,288,128]{2,1,0:T(8,128)(2,1)S(1)}, u32[]{:S(2)}, u32[]{:S(2)}) %collective-permute-start.1) | collective-permute-done | bytes 516128 | tf_op jit(solution)/shard_map/ppermute | solution.py:470
  29.8 0.0 copy-start.1
  29.8 0.0 copy-done
  29.8 0.8 copy-done.1
  30.6 37.3 %residual.1 = (f32[52,288,128]{2,1,0:T(8,128)}, f32[50,288,128]{2,1,0:T(8,128)}, f32[54,288,128]{2,1,0:T(8,128)}, f32[52,288,128]{2,1,0:T(8,128)}, f32[2,8,128]{2,1,0:T(8,128)}) custom-call(s32[3]{0:T(128)} %pad_add_fusion.spot, s32[1,64]{1,0:T(1,128)} %columns.1, bf16[48,288,128]{2,1,0:T(8,128)(2,1)} %logk.1, bf16[48,288,128]{2,1,0:T(8,128)(2,1)} %bitcast.22, ...), custom_call_target="tpu_custom_call" | custom-call | tf_op jit(solution)/shard_map/residual/pallas_call | solution.py:472
  67.9 0.8 reduce_sum.18
  68.7 9.9 %psum.14 = f32[2]{0:T(128)S(1)} all-reduce(f32[2]{0:T(128)S(1)} %reduce_sum.18), channel_id=1, replica_groups=mesh['groups'=2,'space'=4,'test'=4] {'space'}, use_global_device_ids=true, to_apply=%region_1.0 | all-reduce | flops 2 | bytes 16 | tf_op jit(solution)/shard_map/psum | solution.py:454
  78.6 0.6 fusion.25
  80.6 19.0 %second.1 = f32[2,8,128]{2,1,0:T(8,128)} custom-call(f32[1]{0:T(128)} %bitcast.10.scalars, f32[52,288,128]{2,1,0:T(8,128)} %get-tuple-element.13.start, f32[50,288,128]{2,1,0:T(8,128)} %get-tuple-element.14.image, f32[54,288,128]{2,1,0:T(8,128)} %get-tuple-element.15.soft, f32[52,288,128]{2,1,0:T(8,128)} %get-tuple-element.16.around), custom_call_target="tpu_custom_call" | custom-call | tf_op jit(solution)/shard_map/second/pallas_call | solution.py:489
  99.6 0.8 reduce_sum.19
  100.4 0.9 sine_add_fusion.1.cas
  101.3 9.0 %psum.15 = f32[2]{0:T(128)S(1)} all-reduce(f32[2]{0:T(128)S(1)} %reduce_sum.19), channel_id=1, replica_groups=mesh['groups'=2,'space'=4,'test'=4] {'space'}, use_global_device_ids=true, to_apply=%region_3.0 | all-reduce | flops 2 | bytes 16 | tf_op jit(solution)/shard_map/psum | solution.py:454
  110.3 0.7 fusion.24
  115.6 0.7 pad_maximum_fusion.2.scalars
  116.2 37.1 %gradient.1 = f32[4,12,288,128]{3,2,1,0:T(8,128)} custom-call(s32[3]{0:T(128)} %pad_add_fusion.spot, f32[2]{0:T(128)} %pad_maximum_fusion.2.scalars, bf16[48,288,128]{2,1,0:T(8,128)(2,1)} %bitcast.23, bf16[48,288,128]{2,1,0:T(8,128)(2,1)} %bitcast.24, bf16[7,288,128]{2,1,0:T(8,128)(2,1)} %copy-done, bf16[7,288,128]{2,1,0:T(8,128)(2,1)} %copy-done.1, ...), custom_call_target="tpu_custom_call" | custom-call | tf_op jit(solution)/shard_map/gradient/pallas_call | solution.py:504
  153.3 0.0 reduce-scatter.2.cloned.1.call-update
  153.4 2.5 sine_add_fusion.cas
  156.0 0.8 add_divide_fusion.1.rho
  156.8 0.2 fusion.15
  156.9 0.2 divide_dynamic-update-slice_fusion
  157.1 0.2 fusion.14
  157.3 0.2 fusion.11
  157.5 0.2 fusion.13
  157.7 0.2 fusion.12.tables
  158.0 0.0 copy-start.2
  158.0 58.1 %reduce-scatter.2.cloned.1.call-done = f32[1,12,288,128]{3,2,1,0:T(8,128)} async-done(((f32[4,12,288,128]{3,2,1,0:T(8,128)}), f32[1,12,288,128]{3,2,1,0:T(8,128)}) %reduce-scatter.2.cloned.1.call-update) | async-done | bytes 1769488 | tf_op jit(solution)/shard_map/reduce_scatter | solution.py:513
  216.1 11.9 %moment.1 = (f32[48,72,128]{2,1,0:T(8,128)}, f32[4,72,128]{2,1,0:T(8,128)}) custom-call(f32[12,288,128]{2,1,0:T(8,128)} %bitcast.26, f32[288,288]{1,0:T(8,128)} %sine_add_fusion.cas, f32[72,128]{1,0:T(8,128)} %add_divide_fusion.1.rho), custom_call_target="tpu_custom_call" | custom-call | tf_op jit(solution)/shard_map/moment/pallas_call | solution.py:532
  228.0 19.0 %all-gather = f32[16,72,128]{2,1,0:T(8,128)} all-gather(f32[4,72,128]{2,1,0:T(8,128)} %get-tuple-element.18), channel_id=2, replica_groups=mesh['groups'=2,'space'=4,'test'=4] {'space'}, dimensions={0}, use_global_device_ids=true | all-gather | bytes 737280 | tf_op jit(solution)/shard_map/all_gather | solution.py:540
  247.0 0.0 copy-done.2
  247.0 12.3 %filter.1 = f32[4,12,72,128]{3,2,1,0:T(8,128)} custom-call(s32[1]{0:T(128)} %bitcast.where_at, f32[48,72,128]{2,1,0:T(8,128)} %get-tuple-element.17.freq, f32[4,4,72,128]{3,2,1,0:T(8,128)} %bitcast.25, f32[6,72,128]{2,1,0:T(8,128)} %copy-done.2, f32[288,288]{1,0:T(8,128)} %sine_add_fusion.cas), custom_call_target="tpu_custom_call" | custom-call | tf_op jit(solution)/shard_map/filter/pallas_call | solution.py:541
  259.4 26.6 %all_to_all.5.received = f32[4,12,72,128]{3,2,1,0:T(8,128)} all-to-all(f32[4,12,72,128]{3,2,1,0:T(8,128)} %filter.1), channel_id=1, replica_groups=mesh['groups'=2,'space'=4,'test'=4] {'test'}, dimensions={0} | all-to-all | bytes 3538944 | tf_op jit(solution)/shard_map/all_to_all | solution.py:550
  286.0 8.2 %depth.1 = f32[48,72,128]{2,1,0:T(8,128)} custom-call(f32[4,12,72,128]{3,2,1,0:T(8,128)} %all_to_all.5.received, f32[128,128]{1,0:T(8,128)} %sine_add_fusion.1.cas), custom_call_target="tpu_custom_call" | custom-call | tf_op jit(solution)/shard_map/depth/pallas_call | solution.py:551
  (2 shorter events, 0.1 us)
Async XLA Ops:
  6.5 209.6 %reduce-scatter.2.cloned.1.call-start = ((), (), s32[]{:S(2)}) async-start(), calls=%async_computation.2 | async-start | bytes 8847360 | tf_op jit(solution)/shard_map/reduce_scatter | solution.py:513
  9.7 15.9 %collective-permute-start = (bf16[7,288,128]{2,1,0:T(8,128)(2,1)S(1)}, bf16[7,288,128]{2,1,0:T(8,128)(2,1)S(1)}, u32[]{:S(2)}, u32[]{:S(2)}) collective-permute-start(bf16[7,288,128]{2,1,0:T(8,128)(2,1)S(1)} %pad_maximum_fusion), channel_id=1, source_target_pairs={{0,4},{4,8},{8,12},{1,5},{5,9},{9,13},{2,6},{6,10},{10,14},{3,7},{... | collective-permute-start | bytes 1548296 | tf_op jit(solution)/shard_map/ppermute | solution.py:469
  14.7 15.1 %collective-permute-start.1 = (bf16[7,288,128]{2,1,0:T(8,128)(2,1)S(1)}, bf16[7,288,128]{2,1,0:T(8,128)(2,1)S(1)}, u32[]{:S(2)}, u32[]{:S(2)}) collective-permute-start(bf16[7,288,128]{2,1,0:T(8,128)(2,1)S(1)} %pad_maximum_fusion.1), channel_id=1, source_target_pairs={{4,0},{8,4},{12,8},{5,1},{9,5},{13,9},{6,2},{10,6},{14,10},{7,3},{... | collective-permute-start | bytes 1548296 | tf_op jit(solution)/shard_map/ppermute | solution.py:470
  25.6 4.2 %copy-start = (bf16[7,288,128]{2,1,0:T(8,128)(2,1)}, bf16[7,288,128]{2,1,0:T(8,128)(2,1)S(1)}, u32[]{:S(2)}) copy-start(bf16[7,288,128]{2,1,0:T(8,128)(2,1)S(1)} %collective-permute-done.before) | copy-start | bytes 1548292
  29.8 0.8 copy-start.1
  158.0 89.1 %copy-start.2 = (f32[6,72,128]{2,1,0:T(8,128)}, f32[6,72,128]{2,1,0:T(8,128)S(1)}, u32[]{:S(2)}) copy-start(f32[6,72,128]{2,1,0:T(8,128)S(1)} %fusion.12.tables) | copy-start | bytes 663556
Sparse Core Ops, SparseCore 0:
  153.5 62.6 reduce-scatter.1

commit v2 on v1

--- a/solution.py
+++ b/solution.py
@@ -1,5 +1,3 @@
-import functools
-
 import jax
 import jax.numpy as jnp
 from jax import lax
@@ -317,10 +315,44 @@
     return upper + lower
 
 
+MESH = pl.DeviceIdType.MESH
+
+
+def greet(others):
+    barrier = pltpu.get_barrier_semaphore()
+    for other in others:
+        pl.semaphore_signal(barrier, inc=1, device_id=other, device_id_type=MESH)
+    pl.semaphore_wait(barrier, len(others))
+
+
 def gradient_kernel(
-    spot, scalars, warm, heads, before, after, start, image, soft, cas, out, field, head
+    spot,
+    scalars,
+    warm,
+    heads,
+    before,
+    after,
+    start,
+    image,
+    soft,
+    cas,
+    out,
+    field,
+    head,
+    mine,
+    from_mate,
+    from_across,
+    send_mate,
+    take_mate,
+    send_across,
+    take_across,
 ):
     rows, width, depth = warm.shape
+    here = lax.axis_index("test")
+    half, core = here // 2, lax.rem(here, 2)
+    mate = {"test": 2 * half + 1 - core}
+    across = {"test": 2 * (1 - half) + core}
+    greet([mate, across])
     first_row = spot[0]
     well = spot[2]
     with_start, with_image = scalars[0], scalars[1]
@@ -329,7 +361,7 @@
         field[to] = (
             warm_row.astype(jnp.float32) + with_start * start[to + 1] - with_image * image[to]
         )
-        head[to] = head_row.astype(jnp.float32)
+        head[to] = head_row
 
     fill(0, before[5], before[6])
     fill(rows + 1, after[3], after[6])
@@ -340,39 +372,104 @@
 
     lax.fori_loop(0, rows, middle, 0)
     at_row = iotas((width, depth))[0]
-    count = out.shape[0]
+    count = 4
+    groups = rows // count
 
     def term(i):
-        s, f, h = soft[i + 3], field[i + 1], head[i + 1]
+        s, f, h = soft[i + 3], field[i + 1], head[i + 1].astype(jnp.float32)
         gathered = face_terms(s, f, h, 0) + face_terms(s, f, h, 1)
-        gathered += soft[i + 2] * ((f - field[i]) * (h - head[i]))
-        gathered += soft[i + 4] * ((f - field[i + 2]) * (h - head[i + 2]))
+        gathered += soft[i + 2] * ((f - field[i]) * (h - head[i].astype(jnp.float32)))
+        gathered += soft[i + 4] * ((f - field[i + 2]) * (h - head[i + 2].astype(jnp.float32)))
         keep = at_row != well - (first_row + i) * width
         value = jnp.where(keep, -0.5 * s * gathered, 0.0)
         return jnp.dot(value, cas[...], precision=HIGHEST, preferred_element_type=jnp.float32)
 
-    def group(g, _):
+    def to_mate(g):
+        return pltpu.make_async_remote_copy(
+            src_ref=mine.at[1 - core, g],
+            dst_ref=from_mate.at[g],
+            send_sem=send_mate.at[g],
+            recv_sem=take_mate.at[g],
+            device_id=mate,
+            device_id_type=MESH,
+        )
+
+    def to_across(g):
+        return pltpu.make_async_remote_copy(
+            src_ref=mine.at[core, g, 1 - half],
+            dst_ref=from_across.at[g],
+            send_sem=send_across.at[g],
+            recv_sem=take_across.at[g],
+            device_id=across,
+            device_id_type=MESH,
+        )
+
+    def group(g):
         for t, plane in enumerate(swap_blocks([term(g * count + p) for p in range(count)])):
-            out[t, g] = plane
-        return 0
-
-    lax.fori_loop(0, rows // count, group, 0)
-
-
-def moment_kernel(count, summed, cas, rho, freq, moments):
+            mine[t % 2, g, t // 2] = plane
+        to_mate(g).start()
+
+    def relay(g):
+        to_mate(g).wait_recv()
+        mine[core, g, 1 - half] += from_mate[g, 1 - half]
+        to_across(g).start()
+
+    group(0)
+
+    def step(g, _):
+        group(g)
+        relay(g - 1)
+        return 0
+
+    lax.fori_loop(1, groups, step, 0)
+    relay(groups - 1)
+
+    def finish(g, _):
+        to_across(g).wait_recv()
+        out[g] = (mine[core, g, half] + from_mate[g, half]) + from_across[g]
+        to_mate(g).wait_send()
+        to_across(g).wait_send()
+        return 0
+
+    lax.fori_loop(0, groups, finish, 0)
+
+
+def spectral_kernel(
+    summed,
+    tables,
+    cas_across,
+    cas_depth,
+    out,
+    freq,
+    moments,
+    filtered,
+    going,
+    coming,
+    send_end,
+    take_end,
+    send_back,
+    take_back,
+):
     groups, width, lanes = summed.shape
-    part = width // count
-
-    def across(g, _):
-        mixed = jnp.dot(cas[...], summed[g], precision=HIGHEST, preferred_element_type=jnp.float32)
+    count, part = going.shape[0], going.shape[2]
+    rows = groups * count
+    slabs = moments.shape[0]
+    slab, here = lax.axis_index("space"), lax.axis_index("test")
+    others = [{"space": lax.rem(slab + k, slabs)} for k in range(1, slabs)]
+    peers = [lax.rem(here + k, count) for k in range(1, count)]
+    greet(others + [{"test": peer} for peer in peers])
+
+    def mix(g, _):
+        mixed = jnp.dot(
+            cas_across[...], summed[g], precision=HIGHEST, preferred_element_type=jnp.float32
+        )
         blocks = [mixed[j * part : (j + 1) * part] for j in range(count)]
         for p, plane in enumerate(swap_blocks(blocks)):
             freq[g * count + p] = plane
         return 0
 
-    lax.fori_loop(0, groups, across, 0)
-    pole = rho[...]
-    rows = groups * count
+    lax.fori_loop(0, groups, mix, 0)
+    pole, level, slope, decay, wrap_one, wrap_two = (tables[n] for n in range(6))
 
     def walk(i, carry):
         one, two, back_one, back_two = carry
@@ -387,20 +484,27 @@
     zero = jnp.zeros((part, lanes), jnp.float32)
     ends = lax.fori_loop(0, rows, walk, (zero, zero, zero, zero))
     for n in range(4):
-        moments[n] = ends[n]
-
-
-def filter_kernel(count, where_at, freq, moments, tables, cas, out, filtered):
-    rows, part, lanes = freq.shape
-    slabs = moments.shape[0]
-    me = where_at[0]
-    pole, level, slope, decay, wrap_one, wrap_two = (tables[n] for n in range(6))
+        moments[slab, n] = ends[n]
+    copies = [
+        pltpu.make_async_remote_copy(
+            src_ref=moments.at[slab],
+            dst_ref=moments.at[slab],
+            send_sem=send_end.at[k],
+            recv_sem=take_end.at[k],
+            device_id=other,
+            device_id_type=MESH,
+        )
+        for k, other in enumerate(others)
+    ]
+    for copy in copies:
+        copy.start()
+    for copy in copies:
+        copy.wait()
 
     def carried(direction, n):
-        one = jnp.zeros((part, lanes), jnp.float32)
-        two = one
+        one, two = zero, zero
         for m in range(slabs, 0, -1):
-            other = lax.rem(me + 2 * slabs - direction * m, slabs)
+            other = lax.rem(slab + 2 * slabs - direction * m, slabs)
             one, two = (
                 decay * one + moments[other, n],
                 decay * (two + rows * one) + moments[other, n + 1],
@@ -426,24 +530,37 @@
 
     lax.fori_loop(0, rows, backward, carried(-1, 2))
 
-    def across(g, _):
+    def to_peer(k, g):
+        return pltpu.make_async_remote_copy(
+            src_ref=going.at[peers[k], g],
+            dst_ref=coming.at[here, g],
+            send_sem=send_back.at[k, g],
+            recv_sem=take_back.at[k, g],
+            device_id={"test": peers[k]},
+            device_id_type=MESH,
+        )
+
+    def unmix(g, _):
         blocks = swap_blocks([filtered[g * count + p] for p in range(count)])
         stacked = jnp.concatenate(blocks, axis=0)
-        mixed = jnp.dot(cas[...], stacked, precision=HIGHEST, preferred_element_type=jnp.float32)
+        mixed = jnp.dot(
+            cas_across[...], stacked, precision=HIGHEST, preferred_element_type=jnp.float32
+        )
         for u in range(count):
-            out[u, g] = mixed[u * part : (u + 1) * part]
-        return 0
-
-    lax.fori_loop(0, rows // count, across, 0)
-
-
-def depth_kernel(received, cas, out):
-    count, groups, part, lanes = received.shape
+            going[u, g] = mixed[u * part : (u + 1) * part]
+        for k in range(count - 1):
+            to_peer(k, g).start()
+        coming[here, g] = going[here, g]
+        return 0
+
+    lax.fori_loop(0, groups, unmix, 0)
 
     def back(g, _):
-        for p, plane in enumerate(swap_blocks([received[t, g] for t in range(count)])):
+        for k in range(count - 1):
+            to_peer(k, g).wait()
+        for p, plane in enumerate(swap_blocks([coming[t, g] for t in range(count)])):
             out[g * count + p] = jnp.dot(
-                plane, cas[...], precision=HIGHEST, preferred_element_type=jnp.float32
+                plane, cas_depth[...], precision=HIGHEST, preferred_element_type=jnp.float32
             )
         return 0
 
@@ -501,16 +618,25 @@
     scalars = jnp.stack([step + step_next * (1.0 + ratio), step_next * step])
     cas_depth = hartley(depth)
     cas_across = hartley(width)
-    sent = pl.pallas_call(
+    groups = rows // count
+    summed = pl.pallas_call(
         gradient_kernel,
-        out_shape=shape(count, rows // count, width, depth),
+        out_shape=shape(groups, width, depth),
         in_specs=[SM, SM] + [VM] * 8,
         out_specs=VM,
-        scratch_shapes=[pltpu.VMEM((rows + 2, width, depth), jnp.float32)] * 2,
-        compiler_params=BIG,
+        scratch_shapes=[
+            pltpu.VMEM((rows + 2, width, depth), jnp.float32),
+            pltpu.VMEM((rows + 2, width, depth), jnp.bfloat16),
+            pltpu.VMEM((2, groups, 2, width, depth), jnp.float32),
+            pltpu.VMEM((groups, 2, width, depth), jnp.float32),
+            pltpu.VMEM((groups, width, depth), jnp.float32),
+        ]
+        + [pltpu.SemaphoreType.DMA((groups,))] * 4,
+        compiler_params=pltpu.CompilerParams(
+            vmem_limit_bytes=60 * 1024 * 1024, collective_id=1, has_side_effects=True
+        ),
         name="gradient",
     )(spot, scalars, warm, head, before, after, start, image, soft, cas_depth)
-    summed = lax.psum_scatter(sent, "test", scatter_dimension=0)
     lanes_at = jnp.arange(depth)
     across_at = (lanes_at // block)[None, :] * part + jnp.arange(part)[:, None]
     depth_at = lax.axis_index("test") * block + lanes_at % block
@@ -529,40 +655,34 @@
     tables = jnp.stack(
         [pole, level, slope, pole**rows, wrap_one, along * turn * wrap_one * wrap_one]
     )
-    freq, moments = pl.pallas_call(
-        functools.partial(moment_kernel, count),
-        out_shape=[shape(rows, part, depth), shape(4, part, depth)],
-        in_specs=[VM] * 3,
-        out_specs=[VM] * 2,
-        compiler_params=BIG,
-        name="moment",
-    )(summed, cas_across, pole)
-    moments = lax.all_gather(moments, "space")
-    back = pl.pallas_call(
-        functools.partial(filter_kernel, count),
-        out_shape=shape(count, rows // count, part, depth),
-        in_specs=[SM] + [VM] * 4,
+    return pl.pallas_call(
+        spectral_kernel,
+        out_shape=shape(rows, part, depth),
+        in_specs=[VM] * 4,
         out_specs=VM,
-        scratch_shapes=[pltpu.VMEM((rows, part, depth), jnp.float32)],
-        compiler_params=BIG,
-        name="filter",
-    )(lax.axis_index("space").astype(jnp.int32)[None], freq, moments, tables, cas_across)
-    received = lax.all_to_all(back, "test", split_axis=0, concat_axis=0, tiled=True)
-    return pl.pallas_call(
-        depth_kernel,
-        out_shape=shape(rows, part, depth),
-        in_specs=[VM] * 2,
-        out_specs=VM,
-        compiler_params=BIG,
-        name="depth",
-    )(received, cas_depth)
+        scratch_shapes=[
+            pltpu.VMEM((rows, part, depth), jnp.float32),
+            pltpu.VMEM((slabs, 4, part, depth), jnp.float32),
+            pltpu.VMEM((rows, part, depth), jnp.float32),
+            pltpu.VMEM((count, groups, part, depth), jnp.float32),
+            pltpu.VMEM((count, groups, part, depth), jnp.float32),
+            pltpu.SemaphoreType.DMA((slabs - 1,)),
+            pltpu.SemaphoreType.DMA((slabs - 1,)),
+            pltpu.SemaphoreType.DMA((count - 1, groups)),
+            pltpu.SemaphoreType.DMA((count - 1, groups)),
+        ],
+        compiler_params=pltpu.CompilerParams(
+            vmem_limit_bytes=40 * 1024 * 1024, collective_id=2, has_side_effects=True
+        ),
+        name="spectral",
+    )(summed, tables, cas_across, cas_depth)
 
 
 def pick(log_k, *rest):
     rows, width, depth = log_k.shape
     count = lax.axis_size("test")
-    fits = depth == 128 and depth % count == 0 and rows % count == 0 and width % (8 * count) == 0
-    return (fast if fits and rows >= 3 else on_device)(log_k, *rest)
+    fits = depth == 128 and count == 4 and rows % count == 0 and width % (8 * count) == 0
+    return (fast if fits and lax.axis_size("space") > 1 else on_device)(log_k, *rest)
 
 
 def solution(mesh):

time: 302 us -> 219 us (0.73)
  waiting for transfers between devices: 70.7 us -> 11.3 us
  blocking collectives: 64.5 us -> 18.9 us
  Pallas kernels: 126 us -> 159 us
  between operations: 20.2 us -> 6.47 us
    reduce_scatter x1 -> x0, waiting for transfers between devices: 58.1 us -> none  [fast(): summed = lax.psum_scatter(sent, 'test', scatter_dimension=0)]
    pallas_call x4 -> x2, Pallas kernels: 69.5 us -> 102 us  [the longest x1 57.7 us: fast(): pl.pallas_call(gradient_kernel, out_shape=shape(groups, width, depth), in...]
    all_to_all x1 -> x0, blocking collectives: 26.6 us -> none  [fast(): lax.all_to_all(back, 'test', split_axis=0, concat_axis=0, tiled=True)]
    all_gather x1 -> x0, blocking collectives: 19 us -> none  [fast(): moments = lax.all_gather(moments, 'space')]
  transfers between devices with their start and end apart: 3 -> 2, of which waited for: 3 -> 2; matrix products, arithmetic and copies ran while one was open for 2% -> 1% of each run, Pallas kernels for 0% -> 0%
where the time goes in v2:
time: 219 us; the launch traced here: 217 us
  Pallas kernels  159 us (73%)
  blocking collectives  18.9 us (9%)
  waiting for transfers between devices  11.3 us (5%)
  local copies, waits for them, and re-layouts  7.88 us (4%)
  other arithmetic  6.94 us (3%)
  between operations  6.47 us (3%)
  starting transfers between devices  6.25 us (3%)
    pallas_call x1, Pallas kernels, fast(): pl.pallas_call(gradient_kernel, out_shape=shape(groups, width, depth), in...  57.7 us
    pallas_call x1, Pallas kernels, fast(): pl.pallas_call(spectral_kernel, out_shape=shape(rows, part, depth), in_sp...  43.9 us
    pallas_call x1, Pallas kernels, fast(): pl.pallas_call(residual_kernel, out_shape=[shape(rows + 4, width, depth),...  38.2 us
    pallas_call x1, Pallas kernels, fast(): pl.pallas_call(second_kernel, out_shape=shape(2, 8, depth), in_specs=[SM,...  19.2 us
    psum x2, blocking collectives, space_sum(): both = lax.psum(jnp.sum(sums, axis=(1, 2)), 'space')  18.9 us
    ppermute x1, waiting for transfers between devices, fast(): before = lax.ppermute(high, 'space', [(i, i + 1) for i in range(slabs - 1)])  7.05 us
    ppermute x1, starting transfers between devices, fast(): before = lax.ppermute(high, 'space', [(i, i + 1) for i in range(slabs - 1)])  4.96 us
  transfers between devices with their start and end apart: 2, of which 2 were waited for; matrix products, arithmetic and copies ran while one was open for 1% of the time, Pallas kernels for 0%

profile of v2, /device:TPU:0, one launch (start us, length us, event | category | flops | bytes accessed | tf_op | source)
XLA Modules:
  0.0 216.7 jit_solution(7564147998849570553)
XLA Ops:
  0.0 1.1 fusion.23
  1.1 1.1 slice_bitcast_fusion
  2.2 0.9 slice_bitcast_fusion.2
  3.1 0.1 pad_maximum_fusion
  3.2 5.0 %collective-permute-start = (bf16[7,288,128]{2,1,0:T(8,128)(2,1)S(1)}, bf16[7,288,128]{2,1,0:T(8,128)(2,1)S(1)}, u32[]{:S(2)}, u32[]{:S(2)}) collective-permute-start(bf16[7,288,128]{2,1,0:T(8,128)(2,1)S(1)} %pad_maximum_fusion), channel_id=1, source_target_pairs={{0,4},{4,8},{8,12},{1,5},{5,9},{9,13},{2,6},{6,10},{10,14},{3,7},{... | collective-permute-start | bytes 1548296 | tf_op jit(solution)/shard_map/ppermute | solution.py:586
  8.1 0.1 pad_maximum_fusion.1
  8.2 1.3 collective-permute-start.1
  10.2 0.2 fusion.15
  10.4 0.2 divide_dynamic-update-slice_fusion
  10.6 0.2 fusion.14
  10.8 0.2 fusion.11
  11.0 0.6 pad_add_fusion.spot
  11.6 0.2 fusion.13
  11.8 0.2 fusion.12.tables
  12.0 7.0 %collective-permute-done.before = bf16[7,288,128]{2,1,0:T(8,128)(2,1)S(1)} collective-permute-done((bf16[7,288,128]{2,1,0:T(8,128)(2,1)S(1)}, bf16[7,288,128]{2,1,0:T(8,128)(2,1)S(1)}, u32[]{:S(2)}, u32[]{:S(2)}) %collective-permute-start) | collective-permute-done | bytes 516128 | tf_op jit(solution)/shard_map/ppermute | solution.py:586
  19.1 0.0 copy-start.2
  19.1 4.2 %collective-permute-done.1.after = bf16[7,288,128]{2,1,0:T(8,128)(2,1)S(1)} collective-permute-done((bf16[7,288,128]{2,1,0:T(8,128)(2,1)S(1)}, bf16[7,288,128]{2,1,0:T(8,128)(2,1)S(1)}, u32[]{:S(2)}, u32[]{:S(2)}) %collective-permute-start.1) | collective-permute-done | bytes 516128 | tf_op jit(solution)/shard_map/ppermute | solution.py:587
  23.3 0.0 copy-start.3
  23.3 0.0 copy-done.2
  23.3 0.8 copy-done.3
  24.1 38.2 %residual.1 = (f32[52,288,128]{2,1,0:T(8,128)}, f32[50,288,128]{2,1,0:T(8,128)}, f32[54,288,128]{2,1,0:T(8,128)}, f32[52,288,128]{2,1,0:T(8,128)}, f32[2,8,128]{2,1,0:T(8,128)}) custom-call(s32[3]{0:T(128)} %pad_add_fusion.spot, s32[1,64]{1,0:T(1,128)} %columns.1, bf16[48,288,128]{2,1,0:T(8,128)(2,1)} %logk.1, bf16[48,288,128]{2,1,0:T(8,128)(2,1)} %bitcast.19, ...), custom_call_target="tpu_custom_call" | custom-call | tf_op jit(solution)/shard_map/residual/pallas_call | solution.py:589
  62.3 0.8 reduce_sum.18
  63.1 1.8 sine_add_fusion.cas_across
  64.9 9.9 %psum.14 = f32[2]{0:T(128)S(1)} all-reduce(f32[2]{0:T(128)S(1)} %reduce_sum.18), channel_id=1, replica_groups=mesh['groups'=2,'space'=4,'test'=4] {'space'}, use_global_device_ids=true, to_apply=%region_1.0 | all-reduce | flops 2 | bytes 16 | tf_op jit(solution)/shard_map/psum | solution.py:571
  74.8 0.7 fusion.25
  76.8 19.2 %second.1 = f32[2,8,128]{2,1,0:T(8,128)} custom-call(f32[1]{0:T(128)} %bitcast.9.scalars, f32[52,288,128]{2,1,0:T(8,128)} %get-tuple-element.11.start, f32[50,288,128]{2,1,0:T(8,128)} %get-tuple-element.12.image, f32[54,288,128]{2,1,0:T(8,128)} %get-tuple-element.13.soft, f32[52,288,128]{2,1,0:T(8,128)} %get-tuple-element.14.around), custom_call_target="tpu_custom_call" | custom-call | tf_op jit(solution)/shard_map/second/pallas_call | solution.py:606
  96.0 0.8 reduce_sum.19
  96.8 0.9 sine_add_fusion.1.cas.cas_depth
  97.7 9.0 %psum.15 = f32[2]{0:T(128)S(1)} all-reduce(f32[2]{0:T(128)S(1)} %reduce_sum.19), channel_id=1, replica_groups=mesh['groups'=2,'space'=4,'test'=4] {'space'}, use_global_device_ids=true, to_apply=%region_3.0 | all-reduce | flops 2 | bytes 16 | tf_op jit(solution)/shard_map/psum | solution.py:571
  106.7 0.7 fusion.24
  111.7 0.7 pad_maximum_fusion.2.scalars
  112.4 0.0 copy-start.1
  112.4 57.7 %gradient.1.summed = f32[12,288,128]{2,1,0:T(8,128)} custom-call(s32[3]{0:T(128)} %pad_add_fusion.spot, f32[2]{0:T(128)} %pad_maximum_fusion.2.scalars, bf16[48,288,128]{2,1,0:T(8,128)(2,1)} %bitcast.20, bf16[48,288,128]{2,1,0:T(8,128)(2,1)} %bitcast.21, bf16[7,288,128]{2,1,0:T(8,128)(2,1)} %copy-done.2, bf16[7,288,128]{2,1,0:T(8,128)(2,1)} %copy-done.3, ...), custom_call_target="tpu_custom_call" | custom-call | tf_op jit(solution)/shard_map/gradient/pallas_call | solution.py:622
  170.1 0.0 copy-done.1
  170.1 0.0 copy-start
  170.2 1.5 copy-done
  171.6 43.9 %spectral.1 = f32[48,72,128]{2,1,0:T(8,128)S(1)} custom-call(f32[12,288,128]{2,1,0:T(8,128)S(1)} %copy-done, f32[6,72,128]{2,1,0:T(8,128)S(1)} %fusion.12.tables, f32[288,288]{1,0:T(8,128)S(1)} %sine_add_fusion.cas_across, f32[128,128]{1,0:T(8,128)S(1)} %copy-done.1), custom_call_target="tpu_custom_call" | custom-call | tf_op jit(solution)/shard_map/spectral/pallas_call | solution.py:658
  215.5 1.2 copy.14
  (2 shorter events, 0.1 us)
Async XLA Ops:
  3.2 15.9 %collective-permute-start = (bf16[7,288,128]{2,1,0:T(8,128)(2,1)S(1)}, bf16[7,288,128]{2,1,0:T(8,128)(2,1)S(1)}, u32[]{:S(2)}, u32[]{:S(2)}) collective-permute-start(bf16[7,288,128]{2,1,0:T(8,128)(2,1)S(1)} %pad_maximum_fusion), channel_id=1, source_target_pairs={{0,4},{4,8},{8,12},{1,5},{5,9},{9,13},{2,6},{6,10},{10,14},{3,7},{... | collective-permute-start | bytes 1548296 | tf_op jit(solution)/shard_map/ppermute | solution.py:586
  8.2 15.1 %collective-permute-start.1 = (bf16[7,288,128]{2,1,0:T(8,128)(2,1)S(1)}, bf16[7,288,128]{2,1,0:T(8,128)(2,1)S(1)}, u32[]{:S(2)}, u32[]{:S(2)}) collective-permute-start(bf16[7,288,128]{2,1,0:T(8,128)(2,1)S(1)} %pad_maximum_fusion.1), channel_id=1, source_target_pairs={{4,0},{8,4},{12,8},{5,1},{9,5},{13,9},{6,2},{10,6},{14,10},{7,3},{... | collective-permute-start | bytes 1548296 | tf_op jit(solution)/shard_map/ppermute | solution.py:587
  19.1 4.2 %copy-start.2 = (bf16[7,288,128]{2,1,0:T(8,128)(2,1)}, bf16[7,288,128]{2,1,0:T(8,128)(2,1)S(1)}, u32[]{:S(2)}) copy-start(bf16[7,288,128]{2,1,0:T(8,128)(2,1)S(1)} %collective-permute-done.before) | copy-start | bytes 1548292
  23.3 0.8 copy-start.3
  112.4 57.8 %copy-start.1 = (f32[128,128]{1,0:T(8,128)S(1)}, f32[128,128]{1,0:T(8,128)}, u32[]{:S(2)}) copy-start(f32[128,128]{1,0:T(8,128)} %sine_add_fusion.1.cas.cas_depth) | copy-start | bytes 196612
  170.1 1.5 copy-start

commit v3 on v2

--- a/solution.py
+++ b/solution.py
@@ -1,5 +1,6 @@
 import jax
 import jax.numpy as jnp
+import numpy as np
 from jax import lax
 from jax.experimental import pallas as pl
 from jax.experimental.pallas import tpu as pltpu
@@ -206,7 +207,7 @@
 
 
 def residual_kernel(
-    spot, columns, logk, warm, before, after, observed, start, image, soft, around, sums, weighted
+    spot, columns, logk, warm, before, after, observed, start, image, soft, sums, weighted, around
 ):
     rows, width, depth = logk.shape
     first_row, last_row = spot[0], spot[1]
@@ -280,30 +281,6 @@
     sums[1] = total_rq
 
 
-def second_kernel(scalars, start, image, soft, around, sums, weighted):
-    rows = start.shape[0] - 4
-    step = scalars[0]
-
-    def scale(i, _):
-        weighted[i] = soft[i + 2] * (start[i + 1] - step * image[i])
-        return 0
-
-    lax.fori_loop(0, rows + 2, scale, 0)
-
-    def apply(i, carry):
-        total_rr, total_rq = carry
-        held = weighted[i + 1]
-        beside = ring_sum(held, 0.0) + (weighted[i] + weighted[i + 2])
-        value = start[i + 2] - step * image[i + 1]
-        applied = held * around[i + 2] - soft[i + 3] * beside
-        return total_rr + plane_total(value * value), total_rq + plane_total(value * applied)
-
-    zero = jnp.zeros((8, start.shape[2]), jnp.float32)
-    total_rr, total_rq = lax.fori_loop(0, rows, apply, (zero, zero))
-    sums[0] = total_rr
-    sums[1] = total_rq
-
-
 def face_terms(soft, field, head, axis):
     size = soft.shape[axis]
     at = iotas(soft.shape)[axis]
@@ -327,7 +304,7 @@
 
 def gradient_kernel(
     spot,
-    scalars,
+    sums,
     warm,
     heads,
     before,
@@ -346,28 +323,96 @@
     take_mate,
     send_across,
     take_across,
+    shared,
+    send_sum,
+    take_sum,
 ):
     rows, width, depth = warm.shape
+    slabs = shared.shape[1]
+    slab = lax.axis_index("space")
+    others = [{"space": lax.rem(slab + k, slabs)} for k in range(1, slabs)]
     here = lax.axis_index("test")
     half, core = here // 2, lax.rem(here, 2)
     mate = {"test": 2 * half + 1 - core}
     across = {"test": 2 * (1 - half) + core}
-    greet([mate, across])
+    greet(others + [mate, across])
     first_row = spot[0]
     well = spot[2]
-    with_start, with_image = scalars[0], scalars[1]
-
-    def fill(to, warm_row, head_row):
+
+    def share(turn):
+        return [
+            pltpu.make_async_remote_copy(
+                src_ref=shared.at[turn, slab],
+                dst_ref=shared.at[turn, slab],
+                send_sem=send_sum.at[turn, k],
+                recv_sem=take_sum.at[turn, k],
+                device_id=other,
+                device_id_type=MESH,
+            )
+            for k, other in enumerate(others)
+        ]
+
+    def gathered_sum(turn, n):
+        total = shared[turn, 0, n]
+        for m in range(1, slabs):
+            total = total + shared[turn, m, n]
+        return jnp.broadcast_to(jnp.sum(total, axis=(0, 1), keepdims=True), (1, depth))
+
+    shared[0, slab] = sums[...]
+    for copy in share(0):
+        copy.start()
+    head[0] = before[6]
+    head[rows + 1] = after[6]
+
+    def keep_head(i, _):
+        head[i + 1] = heads[i]
+        return 0
+
+    lax.fori_loop(0, rows, keep_head, 0)
+    for copy in share(0):
+        copy.wait()
+    norm, curve = gathered_sum(0, 0), gathered_sum(0, 1)
+    length = norm / curve
+
+    def scale(i, _):
+        field[i] = soft[i + 2] * (start[i + 1] - length * image[i])
+        return 0
+
+    lax.fori_loop(0, rows + 2, scale, 0)
+
+    def apply(i, carry):
+        total_rr, total_rq = carry
+        held = field[i + 1]
+        beside = ring_sum(held, 0.0) + (field[i] + field[i + 2])
+        near = ring_sum(soft[i + 3], 1.0) + (soft[i + 2] + soft[i + 4])
+        value = start[i + 2] - length * image[i + 1]
+        applied = held * near - soft[i + 3] * beside
+        return total_rr + plane_total(value * value), total_rq + plane_total(value * applied)
+
+    zero = jnp.zeros((8, depth), jnp.float32)
+    total_rr, total_rq = lax.fori_loop(0, rows, apply, (zero, zero))
+    shared[1, slab, 0] = total_rr
+    shared[1, slab, 1] = total_rq
+    for copy in share(1):
+        copy.start()
+    for copy in share(1):
+        copy.wait()
+    norm_next, curve_next = gathered_sum(1, 0), gathered_sum(1, 1)
+    ratio = norm_next / norm
+    length_next = norm_next / (curve_next - ratio * norm_next / length)
+    with_start = length + length_next * (1.0 + ratio)
+    with_image = length_next * length
+
+    def fill(to, warm_row):
         field[to] = (
             warm_row.astype(jnp.float32) + with_start * start[to + 1] - with_image * image[to]
         )
-        head[to] = head_row
-
-    fill(0, before[5], before[6])
-    fill(rows + 1, after[3], after[6])
+
+    fill(0, before[5])
+    fill(rows + 1, after[3])
 
     def middle(i, _):
-        fill(i + 1, warm[i], heads[i])
+        fill(i + 1, warm[i])
         return 0
 
     lax.fori_loop(0, rows, middle, 0)
@@ -567,9 +612,10 @@
     lax.fori_loop(0, groups, back, 0)
 
 
-def space_sum(sums):
-    both = lax.psum(jnp.sum(sums, axis=(1, 2)), "space")
-    return both[0], both[1]
+def table(length):
+    indices = np.arange(length)
+    angles = (indices[:, None] * indices[None, :] % length) * (2.0 * np.pi / length)
+    return jnp.asarray((np.cos(angles) + np.sin(angles)).astype(np.float32))
 
 
 def fast(log_k, heads, warm_adjoint, obs_columns, obs_residuals, well_columns):
@@ -586,43 +632,30 @@
     before = lax.ppermute(high, "space", [(i, i + 1) for i in range(slabs - 1)])
     after = lax.ppermute(low, "space", [(i + 1, i) for i in range(slabs - 1)])
     spot = jnp.stack([first_row, jnp.int32(along), well_columns[0]]).astype(jnp.int32)
-    start, image, soft, around, sums = pl.pallas_call(
+    start, image, soft, sums = pl.pallas_call(
         residual_kernel,
         out_shape=[
             shape(rows + 4, width, depth),
             shape(rows + 2, width, depth),
             shape(rows + 6, width, depth),
-            shape(rows + 4, width, depth),
             shape(2, 8, depth),
         ],
         in_specs=[SM, SM, VM, VM, VM, VM, VM],
-        out_specs=[VM] * 5,
-        scratch_shapes=[pltpu.VMEM((rows + 6, width, depth), jnp.float32)],
+        out_specs=[VM] * 4,
+        scratch_shapes=[
+            pltpu.VMEM((rows + 6, width, depth), jnp.float32),
+            pltpu.VMEM((rows + 4, width, depth), jnp.float32),
+        ],
         compiler_params=BIG,
         name="residual",
     )(spot, obs_columns, log_k, warm, before, after, obs_residuals[0])
-    norm, curve = space_sum(sums)
-    step = norm / curve
-    sums = pl.pallas_call(
-        second_kernel,
-        out_shape=shape(2, 8, depth),
-        in_specs=[SM, VM, VM, VM, VM],
-        out_specs=VM,
-        scratch_shapes=[pltpu.VMEM((rows + 2, width, depth), jnp.float32)],
-        compiler_params=BIG,
-        name="second",
-    )(step[None], start, image, soft, around)
-    norm_next, curve_next = space_sum(sums)
-    ratio = norm_next / norm
-    step_next = norm_next / (curve_next - ratio * norm_next / step)
-    scalars = jnp.stack([step + step_next * (1.0 + ratio), step_next * step])
-    cas_depth = hartley(depth)
-    cas_across = hartley(width)
+    cas_depth = table(depth)
+    cas_across = table(width)
     groups = rows // count
     summed = pl.pallas_call(
         gradient_kernel,
         out_shape=shape(groups, width, depth),
-        in_specs=[SM, SM] + [VM] * 8,
+        in_specs=[SM] + [VM] * 9,
         out_specs=VM,
         scratch_shapes=[
             pltpu.VMEM((rows + 2, width, depth), jnp.float32),
@@ -631,12 +664,14 @@
             pltpu.VMEM((groups, 2, width, depth), jnp.float32),
             pltpu.VMEM((groups, width, depth), jnp.float32),
         ]
-        + [pltpu.SemaphoreType.DMA((groups,))] * 4,
+        + [pltpu.SemaphoreType.DMA((groups,))] * 4
+        + [pltpu.VMEM((2, slabs, 2, 8, depth), jnp.float32)]
+        + [pltpu.SemaphoreType.DMA((2, slabs - 1))] * 2,
         compiler_params=pltpu.CompilerParams(
             vmem_limit_bytes=60 * 1024 * 1024, collective_id=1, has_side_effects=True
         ),
         name="gradient",
-    )(spot, scalars, warm, head, before, after, start, image, soft, cas_depth)
+    )(spot, sums, warm, head, before, after, start, image, soft, cas_depth)
     lanes_at = jnp.arange(depth)
     across_at = (lanes_at // block)[None, :] * part + jnp.arange(part)[:, None]
     depth_at = lax.axis_index("test") * block + lanes_at % block

time: 219 us -> 188 us (0.86)
  blocking collectives: 18.9 us -> 0 us
  between operations: 6.47 us -> 0.78 us
  other arithmetic: 6.94 us -> 2.01 us
    pallas_call x1, Pallas kernels: 57.7 us -> 80.2 us  [fast(): pl.pallas_call(gradient_kernel, out_shape=shape(groups, width, depth), in...]
    pallas_call x1 -> x0, Pallas kernels: 19.2 us -> none  [fast(): pl.pallas_call(second_kernel, out_shape=shape(2, 8, depth), in_specs=[SM,...]
    psum x2 -> x0, blocking collectives: 18.9 us -> none  [space_sum(): both = lax.psum(jnp.sum(sums, axis=(1, 2)), 'space')]
    pallas_call x1, Pallas kernels: 38.2 us -> 34.9 us  [fast(): pl.pallas_call(residual_kernel, out_shape=[shape(rows + 4, width, depth),...]
    add x2 -> x0, other arithmetic: 2.72 us -> none  [hartley(): return jnp.cos(angles) + jnp.sin(angles)]
where the time goes in v3:
time: 188 us; the launch traced here: 186 us
  Pallas kernels  159 us (85%)
  waiting for transfers between devices  11.2 us (6%)
  local copies, waits for them, and re-layouts  6.61 us (4%)
  starting transfers between devices  6.25 us (3%)
  other arithmetic  2.01 us (1%)
    pallas_call x1, Pallas kernels, fast(): pl.pallas_call(gradient_kernel, out_shape=shape(groups, width, depth), in...  80.2 us
    pallas_call x1, Pallas kernels, fast(): pl.pallas_call(spectral_kernel, out_shape=shape(rows, part, depth), in_sp...  44.2 us
    pallas_call x1, Pallas kernels, fast(): pl.pallas_call(residual_kernel, out_shape=[shape(rows + 4, width, depth),...  34.9 us
    ppermute x1, waiting for transfers between devices, fast(): before = lax.ppermute(high, 'space', [(i, i + 1) for i in range(slabs - 1)])  7.01 us
    ppermute x1, starting transfers between devices, fast(): before = lax.ppermute(high, 'space', [(i, i + 1) for i in range(slabs - 1)])  4.96 us
    ppermute x1, waiting for transfers between devices, fast(): after = lax.ppermute(low, 'space', [(i + 1, i) for i in range(slabs - 1)])  4.22 us
  transfers between devices with their start and end apart: 2, of which 2 were waited for; matrix products, arithmetic and copies ran while one was open for 1% of the time, Pallas kernels for 0%

profile of v3, /device:TPU:0, one launch (start us, length us, event | category | flops | bytes accessed | tf_op | source)
XLA Modules:
  0.0 186.2 jit_solution(7563442301088958143)
XLA Ops:
  0.0 1.1 fusion.12
  1.1 1.1 slice_bitcast_fusion
  2.2 0.9 slice_bitcast_fusion.2
  3.1 0.1 pad_maximum_fusion
  3.2 5.0 %collective-permute-start = (bf16[7,288,128]{2,1,0:T(8,128)(2,1)S(1)}, bf16[7,288,128]{2,1,0:T(8,128)(2,1)S(1)}, u32[]{:S(2)}, u32[]{:S(2)}) collective-permute-start(bf16[7,288,128]{2,1,0:T(8,128)(2,1)S(1)} %pad_maximum_fusion), channel_id=1, source_target_pairs={{0,4},{4,8},{8,12},{1,5},{5,9},{9,13},{2,6},{6,10},{10,14},{3,7},{... | collective-permute-start | bytes 1548296 | tf_op jit(solution)/shard_map/ppermute | solution.py:632
  8.1 0.1 pad_maximum_fusion.1
  8.2 1.3 collective-permute-start.1
  10.2 0.2 fusion.4
  10.4 0.2 divide_dynamic-update-slice_fusion
  10.6 0.2 fusion.3
  10.8 0.2 fusion
  11.0 0.7 pad_add_fusion.spot
  11.7 0.2 fusion.2
  11.9 0.2 fusion.1.tables
  12.1 7.0 %collective-permute-done.before = bf16[7,288,128]{2,1,0:T(8,128)(2,1)S(1)} collective-permute-done((bf16[7,288,128]{2,1,0:T(8,128)(2,1)S(1)}, bf16[7,288,128]{2,1,0:T(8,128)(2,1)S(1)}, u32[]{:S(2)}, u32[]{:S(2)}) %collective-permute-start) | collective-permute-done | bytes 516128 | tf_op jit(solution)/shard_map/ppermute | solution.py:632
  19.1 0.0 copy-start.3
  19.1 4.2 %collective-permute-done.1.after = bf16[7,288,128]{2,1,0:T(8,128)(2,1)S(1)} collective-permute-done((bf16[7,288,128]{2,1,0:T(8,128)(2,1)S(1)}, bf16[7,288,128]{2,1,0:T(8,128)(2,1)S(1)}, u32[]{:S(2)}, u32[]{:S(2)}) %collective-permute-start.1) | collective-permute-done | bytes 516128 | tf_op jit(solution)/shard_map/ppermute | solution.py:633
  23.3 0.0 copy-start.4
  23.3 0.0 copy-done.3
  23.3 0.8 copy-done.4
  24.2 34.9 %residual.1 = (f32[52,288,128]{2,1,0:T(8,128)}, f32[50,288,128]{2,1,0:T(8,128)}, f32[54,288,128]{2,1,0:T(8,128)}, f32[2,8,128]{2,1,0:T(8,128)}) custom-call(s32[3]{0:T(128)} %pad_add_fusion.spot, s32[1,64]{1,0:T(1,128)} %columns.1, bf16[48,288,128]{2,1,0:T(8,128)(2,1)} %logk.1, bf16[48,288,128]{2,1,0:T(8,128)(2,1)} %bitcast.12, ...), custom_call_target="tpu_custom_call" | custom-call | tf_op jit(solution)/shard_map/residual/pallas_call | solution.py:635
  59.1 0.0 copy-start.1
  59.1 0.0 copy-start.2
  59.1 80.2 %gradient.1.summed = f32[12,288,128]{2,1,0:T(8,128)} custom-call(s32[3]{0:T(128)} %pad_add_fusion.spot, f32[2,8,128]{2,1,0:T(8,128)} %get-tuple-element.9.sums, bf16[48,288,128]{2,1,0:T(8,128)(2,1)} %bitcast.13, bf16[48,288,128]{2,1,0:T(8,128)(2,1)} %bitcast.14, bf16[7,288,128]{2,1,0:T(8,128)(2,1)} %copy-done.3, bf16[7,288,128]{2,1,0:T(8,128)(2,1)} %copy-done.4, ...), custom_call_target="tpu_custom_call" | custom-call | tf_op jit(solution)/shard_map/gradient/pallas_call | solution.py:655
  139.3 0.0 copy-done.1
  139.3 0.0 copy-done.2
  139.3 0.0 copy-start
  139.3 1.5 copy-done
  140.8 44.2 %spectral.1 = f32[48,72,128]{2,1,0:T(8,128)S(1)} custom-call(f32[12,288,128]{2,1,0:T(8,128)S(1)} %copy-done, f32[6,72,128]{2,1,0:T(8,128)S(1)} %fusion.1.tables, f32[288,288]{1,0:T(8,128)S(1)} %copy-done.1, f32[128,128]{1,0:T(8,128)S(1)} %copy-done.2), custom_call_target="tpu_custom_call" | custom-call | tf_op jit(solution)/shard_map/spectral/pallas_call | solution.py:693
  185.0 1.2 copy.16
  (2 shorter events, 0.1 us)
Async XLA Ops:
  3.2 15.9 %collective-permute-start = (bf16[7,288,128]{2,1,0:T(8,128)(2,1)S(1)}, bf16[7,288,128]{2,1,0:T(8,128)(2,1)S(1)}, u32[]{:S(2)}, u32[]{:S(2)}) collective-permute-start(bf16[7,288,128]{2,1,0:T(8,128)(2,1)S(1)} %pad_maximum_fusion), channel_id=1, source_target_pairs={{0,4},{4,8},{8,12},{1,5},{5,9},{9,13},{2,6},{6,10},{10,14},{3,7},{... | collective-permute-start | bytes 1548296 | tf_op jit(solution)/shard_map/ppermute | solution.py:632
  8.2 15.1 %collective-permute-start.1 = (bf16[7,288,128]{2,1,0:T(8,128)(2,1)S(1)}, bf16[7,288,128]{2,1,0:T(8,128)(2,1)S(1)}, u32[]{:S(2)}, u32[]{:S(2)}) collective-permute-start(bf16[7,288,128]{2,1,0:T(8,128)(2,1)S(1)} %pad_maximum_fusion.1), channel_id=1, source_target_pairs={{4,0},{8,4},{12,8},{5,1},{9,5},{13,9},{6,2},{10,6},{14,10},{7,3},{... | collective-permute-start | bytes 1548296 | tf_op jit(solution)/shard_map/ppermute | solution.py:633
  19.1 4.2 %copy-start.3 = (bf16[7,288,128]{2,1,0:T(8,128)(2,1)}, bf16[7,288,128]{2,1,0:T(8,128)(2,1)S(1)}, u32[]{:S(2)}) copy-start(bf16[7,288,128]{2,1,0:T(8,128)(2,1)S(1)} %collective-permute-done.before) | copy-start | bytes 1548292
  23.3 0.8 copy-start.4
  59.1 80.2 %copy-start.1 = (f32[288,288]{1,0:T(8,128)S(1)}, f32[288,288]{1,0:T(8,128)}, u32[]{:S(2)}) copy-start(f32[288,288]{1,0:T(8,128)} %constant.82.clone.cas_across) | copy-start | bytes 995332
  59.1 80.2 %copy-start.2 = (f32[128,128]{1,0:T(8,128)S(1)}, f32[128,128]{1,0:T(8,128)}, u32[]{:S(2)}) copy-start(f32[128,128]{1,0:T(8,128)} %constant.81.clone.cas.cas_depth) | copy-start | bytes 196612
  139.3 1.5 copy-start

commit v4 on v3

--- a/solution.py
+++ b/solution.py
@@ -158,7 +158,19 @@
     return result * scale_back
 
 
-HIGHEST = lax.Precision.HIGHEST
+def dot3(a, b):
+    def split(x):
+        top = x.astype(jnp.bfloat16)
+        return top, (x - top.astype(jnp.float32)).astype(jnp.bfloat16)
+
+    def dot(x, y):
+        return jnp.dot(x, y, preferred_element_type=jnp.float32)
+
+    a_top, a_low = split(a)
+    b_top, b_low = split(b)
+    return dot(a_top, b_top) + (dot(a_top, b_low) + dot(a_low, b_top))
+
+
 VM = pl.BlockSpec(memory_space=pltpu.VMEM)
 SM = pl.BlockSpec(memory_space=pltpu.SMEM)
 BIG = pltpu.CompilerParams(vmem_limit_bytes=60 * 1024 * 1024)
@@ -427,7 +439,7 @@
         gathered += soft[i + 4] * ((f - field[i + 2]) * (h - head[i + 2].astype(jnp.float32)))
         keep = at_row != well - (first_row + i) * width
         value = jnp.where(keep, -0.5 * s * gathered, 0.0)
-        return jnp.dot(value, cas[...], precision=HIGHEST, preferred_element_type=jnp.float32)
+        return dot3(value, cas[...])
 
     def to_mate(g):
         return pltpu.make_async_remote_copy(
@@ -505,9 +517,7 @@
     greet(others + [{"test": peer} for peer in peers])
 
     def mix(g, _):
-        mixed = jnp.dot(
-            cas_across[...], summed[g], precision=HIGHEST, preferred_element_type=jnp.float32
-        )
+        mixed = dot3(cas_across[...], summed[g])
         blocks = [mixed[j * part : (j + 1) * part] for j in range(count)]
         for p, plane in enumerate(swap_blocks(blocks)):
             freq[g * count + p] = plane
@@ -588,9 +598,7 @@
     def unmix(g, _):
         blocks = swap_blocks([filtered[g * count + p] for p in range(count)])
         stacked = jnp.concatenate(blocks, axis=0)
-        mixed = jnp.dot(
-            cas_across[...], stacked, precision=HIGHEST, preferred_element_type=jnp.float32
-        )
+        mixed = dot3(cas_across[...], stacked)
         for u in range(count):
             going[u, g] = mixed[u * part : (u + 1) * part]
         for k in range(count - 1):
@@ -604,9 +612,7 @@
         for k in range(count - 1):
             to_peer(k, g).wait()
         for p, plane in enumerate(swap_blocks([coming[t, g] for t in range(count)])):
-            out[g * count + p] = jnp.dot(
-                plane, cas_depth[...], precision=HIGHEST, preferred_element_type=jnp.float32
-            )
+            out[g * count + p] = dot3(plane, cas_depth[...])
         return 0
 
     lax.fori_loop(0, groups, back, 0)

time: 188 us -> 185 us (0.984)
  Pallas kernels: 159 us -> 156 us
    pallas_call x1, Pallas kernels: 44.2 us -> 41.3 us  [fast(): pl.pallas_call(spectral_kernel, out_shape=shape(rows, part, depth), in_sp...]
where the time goes in v4:
time: 185 us; the launch traced here: 183 us
  Pallas kernels  156 us (84%)
  waiting for transfers between devices  11.2 us (6%)
  local copies, waits for them, and re-layouts  6.61 us (4%)
  starting transfers between devices  6.25 us (3%)
  other arithmetic  2.01 us (1%)
    pallas_call x1, Pallas kernels, fast(): pl.pallas_call(gradient_kernel, out_shape=shape(groups, width, depth), in...  80 us
    pallas_call x1, Pallas kernels, fast(): pl.pallas_call(spectral_kernel, out_shape=shape(rows, part, depth), in_sp...  41.3 us
    pallas_call x1, Pallas kernels, fast(): pl.pallas_call(residual_kernel, out_shape=[shape(rows + 4, width, depth),...  34.9 us
    ppermute x1, waiting for transfers between devices, fast(): before = lax.ppermute(high, 'space', [(i, i + 1) for i in range(slabs - 1)])  7.01 us
    ppermute x1, starting transfers between devices, fast(): before = lax.ppermute(high, 'space', [(i, i + 1) for i in range(slabs - 1)])  4.96 us
    ppermute x1, waiting for transfers between devices, fast(): after = lax.ppermute(low, 'space', [(i + 1, i) for i in range(slabs - 1)])  4.22 us
  transfers between devices with their start and end apart: 2, of which 2 were waited for; matrix products, arithmetic and copies ran while one was open for 1% of the time, Pallas kernels for 0%

profile of v4, /device:TPU:0, one launch (start us, length us, event | category | flops | bytes accessed | tf_op | source)
XLA Modules:
  0.0 183.2 jit_solution(14901816660691796542)
XLA Ops:
  0.0 1.1 fusion.12
  1.1 1.1 slice_bitcast_fusion
  2.2 0.9 slice_bitcast_fusion.2
  3.1 0.1 pad_maximum_fusion
  3.2 5.0 %collective-permute-start = (bf16[7,288,128]{2,1,0:T(8,128)(2,1)S(1)}, bf16[7,288,128]{2,1,0:T(8,128)(2,1)S(1)}, u32[]{:S(2)}, u32[]{:S(2)}) collective-permute-start(bf16[7,288,128]{2,1,0:T(8,128)(2,1)S(1)} %pad_maximum_fusion), channel_id=1, source_target_pairs={{0,4},{4,8},{8,12},{1,5},{5,9},{9,13},{2,6},{6,10},{10,14},{3,7},{... | collective-permute-start | bytes 1548296 | tf_op jit(solution)/shard_map/ppermute | solution.py:638
  8.1 0.1 pad_maximum_fusion.1
  8.2 1.3 collective-permute-start.1
  10.2 0.2 fusion.4
  10.4 0.2 divide_dynamic-update-slice_fusion
  10.6 0.2 fusion.3
  10.8 0.2 fusion
  11.0 0.7 pad_add_fusion.spot
  11.7 0.2 fusion.2
  11.9 0.2 fusion.1.tables
  12.1 7.0 %collective-permute-done.before = bf16[7,288,128]{2,1,0:T(8,128)(2,1)S(1)} collective-permute-done((bf16[7,288,128]{2,1,0:T(8,128)(2,1)S(1)}, bf16[7,288,128]{2,1,0:T(8,128)(2,1)S(1)}, u32[]{:S(2)}, u32[]{:S(2)}) %collective-permute-start) | collective-permute-done | bytes 516128 | tf_op jit(solution)/shard_map/ppermute | solution.py:638
  19.1 0.0 copy-start.3
  19.1 4.2 %collective-permute-done.1.after = bf16[7,288,128]{2,1,0:T(8,128)(2,1)S(1)} collective-permute-done((bf16[7,288,128]{2,1,0:T(8,128)(2,1)S(1)}, bf16[7,288,128]{2,1,0:T(8,128)(2,1)S(1)}, u32[]{:S(2)}, u32[]{:S(2)}) %collective-permute-start.1) | collective-permute-done | bytes 516128 | tf_op jit(solution)/shard_map/ppermute | solution.py:639
  23.3 0.0 copy-start.4
  23.3 0.0 copy-done.3
  23.3 0.8 copy-done.4
  24.2 34.9 %residual.1 = (f32[52,288,128]{2,1,0:T(8,128)}, f32[50,288,128]{2,1,0:T(8,128)}, f32[54,288,128]{2,1,0:T(8,128)}, f32[2,8,128]{2,1,0:T(8,128)}) custom-call(s32[3]{0:T(128)} %pad_add_fusion.spot, s32[1,64]{1,0:T(1,128)} %columns.1, bf16[48,288,128]{2,1,0:T(8,128)(2,1)} %logk.1, bf16[48,288,128]{2,1,0:T(8,128)(2,1)} %bitcast.12, ...), custom_call_target="tpu_custom_call" | custom-call | tf_op jit(solution)/shard_map/residual/pallas_call | solution.py:641
  59.1 0.0 copy-start.1
  59.1 0.0 copy-start.2
  59.1 80.0 %gradient.1.summed = f32[12,288,128]{2,1,0:T(8,128)} custom-call(s32[3]{0:T(128)} %pad_add_fusion.spot, f32[2,8,128]{2,1,0:T(8,128)} %get-tuple-element.9.sums, bf16[48,288,128]{2,1,0:T(8,128)(2,1)} %bitcast.13, bf16[48,288,128]{2,1,0:T(8,128)(2,1)} %bitcast.14, bf16[7,288,128]{2,1,0:T(8,128)(2,1)} %copy-done.3, bf16[7,288,128]{2,1,0:T(8,128)(2,1)} %copy-done.4, ...), custom_call_target="tpu_custom_call" | custom-call | tf_op jit(solution)/shard_map/gradient/pallas_call | solution.py:661
  139.1 0.0 copy-done.1
  139.2 0.0 copy-done.2
  139.2 0.0 copy-start
  139.2 1.5 copy-done
  140.6 41.3 %spectral.1 = f32[48,72,128]{2,1,0:T(8,128)S(1)} custom-call(f32[12,288,128]{2,1,0:T(8,128)S(1)} %copy-done, f32[6,72,128]{2,1,0:T(8,128)S(1)} %fusion.1.tables, f32[288,288]{1,0:T(8,128)S(1)} %copy-done.1, f32[128,128]{1,0:T(8,128)S(1)} %copy-done.2), custom_call_target="tpu_custom_call" | custom-call | tf_op jit(solution)/shard_map/spectral/pallas_call | solution.py:699
  182.0 1.2 copy.16
  (2 shorter events, 0.1 us)
Async XLA Ops:
  3.2 15.9 %collective-permute-start = (bf16[7,288,128]{2,1,0:T(8,128)(2,1)S(1)}, bf16[7,288,128]{2,1,0:T(8,128)(2,1)S(1)}, u32[]{:S(2)}, u32[]{:S(2)}) collective-permute-start(bf16[7,288,128]{2,1,0:T(8,128)(2,1)S(1)} %pad_maximum_fusion), channel_id=1, source_target_pairs={{0,4},{4,8},{8,12},{1,5},{5,9},{9,13},{2,6},{6,10},{10,14},{3,7},{... | collective-permute-start | bytes 1548296 | tf_op jit(solution)/shard_map/ppermute | solution.py:638
  8.2 15.1 %collective-permute-start.1 = (bf16[7,288,128]{2,1,0:T(8,128)(2,1)S(1)}, bf16[7,288,128]{2,1,0:T(8,128)(2,1)S(1)}, u32[]{:S(2)}, u32[]{:S(2)}) collective-permute-start(bf16[7,288,128]{2,1,0:T(8,128)(2,1)S(1)} %pad_maximum_fusion.1), channel_id=1, source_target_pairs={{4,0},{8,4},{12,8},{5,1},{9,5},{13,9},{6,2},{10,6},{14,10},{7,3},{... | collective-permute-start | bytes 1548296 | tf_op jit(solution)/shard_map/ppermute | solution.py:639
  19.1 4.2 %copy-start.3 = (bf16[7,288,128]{2,1,0:T(8,128)(2,1)}, bf16[7,288,128]{2,1,0:T(8,128)(2,1)S(1)}, u32[]{:S(2)}) copy-start(bf16[7,288,128]{2,1,0:T(8,128)(2,1)S(1)} %collective-permute-done.before) | copy-start | bytes 1548292
  23.3 0.8 copy-start.4
  59.1 80.1 %copy-start.1 = (f32[288,288]{1,0:T(8,128)S(1)}, f32[288,288]{1,0:T(8,128)}, u32[]{:S(2)}) copy-start(f32[288,288]{1,0:T(8,128)} %constant.82.clone.cas_across) | copy-start | bytes 995332
  59.1 80.1 %copy-start.2 = (f32[128,128]{1,0:T(8,128)S(1)}, f32[128,128]{1,0:T(8,128)}, u32[]{:S(2)}) copy-start(f32[128,128]{1,0:T(8,128)} %constant.81.clone.cas.cas_depth) | copy-start | bytes 196612
  139.2 1.5 copy-start
